TPU v7x, 32 devices: a whole 2x2x4 slice. The times are simulated.
32 devices in a mesh: len: 4 (over z), wid: 4 (over y, x), lay: 2 (over core).
Axes of the slice: x: 2, y: 2, z: 4, core: 2. Of those that a mesh axis runs over, the one named last changes fastest.
Arguments:
- displacement: float32 [3, 16, 32, 256], P(None, 'len', 'wid', 'lay'), may hold values from -0.1 to 0.1
- velocity: float32 [3, 16, 32, 256], P(None, 'len', 'wid', 'lay'), may hold values from -1.5 to 1.5
- lame_first: float32 [16, 32, 256], P('len', 'wid', 'lay'), may hold values from 0.5 to 2
- shear_modulus: float32 [16, 32, 256], P('len', 'wid', 'lay'), may hold values from 0.5 to 2
- nodal_mass: float32 [16, 32, 256], P('len', 'wid', 'lay'), may hold values from 1 to 4
- slave_nodes: int32 [4, 4, 2, 64, 128], P('len', 'wid', 'lay'), may hold values from 0 to 4095
- initial_gap: float32 [4, 4, 2, 64, 128], P('len', 'wid', 'lay'), may hold values from -0.15 to 0.1
- candidate: int32 [4, 4, 2, 64, 128], P('len', 'wid', 'lay'), may hold values from 0 to 127
- pair_owner: int32 [4, 4, 2, 64, 1], P('len', 'wid', 'lay'), may hold values from 0 to 15; in each aligned block of 64 rows (0 to 63, 64 to 127, ..., all dimensions but the last counted through in order) at most 8 rows name the same one
- pair_patch: int32 [4, 4, 2, 64], P('len', 'wid', 'lay'), may hold values from 0 to 31
- master_faces: int32 [4, 4, 2, 32, 128], P('len', 'wid', 'lay'), may hold values from 0 to 2943, as said below
Outputs:
- new_displacement: float32 [3, 16, 32, 256], P(None, 'len', 'wid', 'lay')
- new_velocity: float32 [3, 16, 32, 256], P(None, 'len', 'wid', 'lay')
Inputs may be any that keep to these rules, and one draw needn't show every extreme that they name: `slave_nodes`: local node numbers of the device's own block. `candidate`: a face's position within the pair's master patch. `pair_owner`: owners are numbered len index * 4 + wid index and share the device's lay index; among the rows of one device no owner is named more than 8 times, a bound that some block reaches. `pair_patch`: a master patch of the owner. `master_faces`: a face's first node is i * 8 * 128 + j * 128 + k with i < 3 and j < 7, so all 4 of its nodes lie on the owner.
All inputs are finite; a program needn't handle non-finite values.
Results may differ from a plain program's by a relative error of at most 0.00005.
Values sent between devices are 32-bit elements; how exact they have to be, the bound alone decides.
A program may use at most 64 MiB of HBM per device.

v0:
```python
import jax
import jax.numpy as jnp
from jax import lax
from jax.sharding import PartitionSpec as P

STEPS = 2


penalty = 4.0
hourglass = 0.3
time_step = 0.25
corner_offsets = (
    (0, 0, 0),
    (1, 0, 0),
    (0, 1, 0),
    (1, 1, 0),
    (0, 0, 1),
    (1, 0, 1),
    (0, 1, 1),
    (1, 1, 1),
)


def padded_2(cells, sides, width):
    for axis, dim in sides:
        count = lax.axis_size(axis)
        ends = count - 1
        head = lax.slice_in_dim(cells, 0, width, axis=dim)
        tail = lax.slice_in_dim(cells, cells.shape[dim] - width, cells.shape[dim], axis=dim)
        cells = jnp.concatenate(
            [
                lax.ppermute(tail, axis, [(i, (i + 1) % count) for i in range(ends)]),
                cells,
                lax.ppermute(head, axis, [((i + 1) % count, i) for i in range(ends)]),
            ],
            axis=dim,
        )
    return cells


def element_mean(values, counts):
    summed = jnp.zeros(counts, jnp.float32)
    for along_x, along_y, along_z in corner_offsets:
        summed = (
            summed
            + values[
                along_x : along_x + counts[0],
                along_y : along_y + counts[1],
                along_z : along_z + counts[2],
            ]
        )
    return summed * 0.125


def corner_forces(points, lame_elem, shear_elem, counts):
    corners = []
    for along_x, along_y, along_z in corner_offsets:
        corners.append(
            points[
                :,
                along_x : along_x + counts[0],
                along_y : along_y + counts[1],
                along_z : along_z + counts[2],
            ]
        )
    mean_disp = corners[0]
    for corner in corners[1:]:
        mean_disp = mean_disp + corner
    mean_disp = mean_disp * 0.125
    columns = []
    for axis_pos in range(3):
        column = jnp.zeros_like(corners[0])
        for offsets, corner in zip(corner_offsets, corners):
            column = column + (2 * offsets[axis_pos] - 1) * corner
        columns.append(column * 0.25)
    gradient = jnp.stack(columns, axis=1)
    strain_trace = gradient[0, 0] + gradient[1, 1] + gradient[2, 2]
    stress = shear_elem * (gradient + jnp.swapaxes(gradient, 0, 1))
    stress = (
        stress + lame_elem * strain_trace * jnp.eye(3, dtype=jnp.float32)[:, :, None, None, None]
    )
    damping = hourglass * shear_elem
    forces = []
    for offsets, corner in zip(corner_offsets, corners):
        unit_signs = [2 * offsets[0] - 1, 2 * offsets[1] - 1, 2 * offsets[2] - 1]
        traction = (
            unit_signs[0] * stress[:, 0]
            + unit_signs[1] * stress[:, 1]
            + unit_signs[2] * stress[:, 2]
        )
        linear = (
            unit_signs[0] * gradient[:, 0]
            + unit_signs[1] * gradient[:, 1]
            + unit_signs[2] * gradient[:, 2]
        )
        forces.append(-0.25 * traction - damping * (corner - mean_disp - 0.5 * linear))
    return forces


def face_frame(u_flat, node_one, node_two, node_three, node_four):
    at_one = u_flat[:, node_one]
    at_two = u_flat[:, node_two]
    at_three = u_flat[:, node_three]
    at_four = u_flat[:, node_four]
    centroid = (at_one + at_two + at_three + at_four) * 0.25
    shape_tail = (3,) + (1,) * node_one.ndim
    diag_one = at_three - at_one + jnp.array([1.0, 1.0, 0.0], dtype=jnp.float32).reshape(shape_tail)
    diag_two = at_four - at_two + jnp.array([-1.0, 1.0, 0.0], dtype=jnp.float32).reshape(shape_tail)
    normal = jnp.stack(
        [
            diag_one[1] * diag_two[2] - diag_one[2] * diag_two[1],
            diag_one[2] * diag_two[0] - diag_one[0] * diag_two[2],
            diag_one[0] * diag_two[1] - diag_one[1] * diag_two[0],
        ]
    )
    normal = normal / jnp.sqrt(
        normal[0] * normal[0] + normal[1] * normal[1] + normal[2] * normal[2]
    )
    return (centroid, normal)


def contact_terms(centroid, normal, slave_disp, gap_start):
    gap_now = (
        gap_start
        + (slave_disp[0] - centroid[0]) * normal[0]
        + (slave_disp[1] - centroid[1]) * normal[1]
        + (slave_disp[2] - centroid[2]) * normal[2]
    )
    penetration = jnp.minimum(gap_now, 0.0)
    return -penalty * penetration * normal


def valid_rows(length, position, pieces):
    element_low = jnp.arange(length + 1, dtype=jnp.int32) + position * length - 1
    return ((element_low >= 0) & (element_low <= pieces * length - 2)).astype(jnp.float32)


def face_sums(values, chosen_faces):
    row_count, face_count = chosen_faces.shape
    flat_index = (
        jnp.arange(row_count, dtype=jnp.int32)[:, None] * face_count + chosen_faces
    ).reshape(-1)
    summed = (
        jnp.zeros((3, row_count * face_count), jnp.float32)
        .at[:, flat_index]
        .add(values.reshape(3, -1))
    )
    return summed.reshape(3, row_count, face_count).transpose(1, 0, 2)


def route_out(buffer):
    return lax.all_to_all(buffer, ("len", "wid"), split_axis=0, concat_axis=0, tiled=True)


def route_back(buffer):
    return lax.all_to_all(buffer, ("len", "wid"), split_axis=0, concat_axis=0, tiled=True)


def per_device(
    displacement,
    velocity,
    lame_first,
    shear_modulus,
    nodal_mass,
    slave_nodes,
    initial_gap,
    candidate,
    pair_owner,
    pair_patch,
    master_faces,
):
    span_x, span_y, span_z = (displacement.shape[1], displacement.shape[2], displacement.shape[3])
    n_len = lax.axis_size("len")
    n_wid = lax.axis_size("wid")
    groups = n_len * n_wid
    pairs = slave_nodes.shape[3]
    face_count = slave_nodes.shape[4]
    patches = master_faces.shape[3]
    capacity = max(2, 2 * pairs // groups)
    slots = groups * capacity
    node_count = span_x * span_y * span_z
    slaves = slave_nodes.reshape(pairs, face_count)
    gaps = initial_gap.reshape(pairs, face_count)
    chosen = candidate.reshape(pairs, face_count)
    owners = pair_owner.reshape(pairs)
    wanted = pair_patch.reshape(pairs)
    node_one = master_faces.reshape(patches, face_count)
    node_two = node_one + span_y * span_z
    node_three = node_one + span_y * span_z + span_z
    node_four = node_one + span_z
    member = (owners[:, None] == jnp.arange(groups, dtype=jnp.int32)[None, :]).astype(jnp.int32)
    before = jnp.cumsum(member, axis=0) - member
    rank_in = jnp.sum(before * member, axis=1)
    slot_index = owners * capacity + rank_in
    request = jnp.full((slots,), -1, jnp.int32).at[slot_index].set(wanted).reshape(groups, capacity)
    stacked = jnp.stack([lame_first, shear_modulus])
    rim = padded_2(stacked, (("len", 1), ("wid", 2), ("lay", 3)), 1)
    counts = (span_x + 1, span_y + 1, span_z + 1)
    mask_x = valid_rows(span_x, lax.axis_index("len"), n_len)
    mask_y = valid_rows(span_y, lax.axis_index("wid"), n_wid)
    mask_z = valid_rows(span_z, lax.axis_index("lay"), lax.axis_size("lay"))
    mask_all = mask_x[:, None, None] * mask_y[None, :, None] * mask_z[None, None, :]
    lame_elem = element_mean(rim[0], counts) * mask_all
    shear_elem = element_mean(rim[1], counts) * mask_all
    incoming = lax.all_to_all(request, ("len", "wid"), split_axis=0, concat_axis=0, tiled=True)
    incoming_flat = incoming.reshape(slots)
    live = incoming_flat >= 0
    safe_ids = jnp.maximum(incoming_flat, 0)
    patch_onehot = (
        (safe_ids[None, :] == jnp.arange(patches, dtype=jnp.int32)[:, None]) & live[None, :]
    ).astype(jnp.float32)
    for step in range(STEPS):
        padded = padded_2(displacement, (("len", 1), ("wid", 2), ("lay", 3)), 1)
        forces = corner_forces(padded, lame_elem, shear_elem, counts)
        internal = jnp.zeros((3, span_x, span_y, span_z), jnp.float32)
        for offsets, force in zip(corner_offsets, forces):
            internal = (
                internal
                + force[
                    :,
                    1 - offsets[0] : 1 - offsets[0] + span_x,
                    1 - offsets[1] : 1 - offsets[1] + span_y,
                    1 - offsets[2] : 1 - offsets[2] + span_z,
                ]
            )
        u_flat = displacement.reshape(3, -1)
        centroid, normal = face_frame(u_flat, node_one, node_two, node_three, node_four)
        table = jnp.concatenate([centroid, normal], axis=0).transpose(1, 0, 2)
        slave_disp = u_flat[:, slaves]
        tiles = table[safe_ids] * live[:, None, None].astype(jnp.float32)
        arrived = route_out(tiles.reshape(groups, capacity, 6, face_count))
        mine = arrived.reshape(slots, 6, face_count)[slot_index]
        picked = jnp.take_along_axis(
            mine, jnp.broadcast_to(chosen[:, None, :], (pairs, 6, face_count)), axis=2
        )
        slave_part = contact_terms(
            picked[:, 0:3].transpose(1, 0, 2), picked[:, 3:6].transpose(1, 0, 2), slave_disp, gaps
        )
        reaction = face_sums(-slave_part, chosen)
        back_buffer = jnp.zeros((slots, 3, face_count), jnp.float32).at[slot_index].set(reaction)
        returned = route_back(back_buffer.reshape(groups, capacity, 3, face_count)).reshape(
            slots, 3 * face_count
        )
        patch_react = jnp.dot(
            patch_onehot,
            returned,
            precision=lax.Precision.HIGHEST,
            preferred_element_type=jnp.float32,
        )
        quarter = 0.25 * patch_react.reshape(patches, 3, face_count).transpose(1, 0, 2)
        contact = jnp.zeros((3, node_count), jnp.float32).at[:, slaves].add(slave_part)
        contact = contact.at[:, node_one].add(quarter)
        contact = contact.at[:, node_two].add(quarter)
        contact = contact.at[:, node_three].add(quarter)
        contact = contact.at[:, node_four].add(quarter)
        total_force = internal + contact.reshape(3, span_x, span_y, span_z)
        velocity = velocity + time_step * total_force / nodal_mass[None]
        displacement = displacement + time_step * velocity
    return (displacement, velocity)


def solution(mesh):
    in_specs = (
        P(None, "len", "wid", "lay"),
        P(None, "len", "wid", "lay"),
        P("len", "wid", "lay"),
        P("len", "wid", "lay"),
        P("len", "wid", "lay"),
        P("len", "wid", "lay", None, None),
        P("len", "wid", "lay", None, None),
        P("len", "wid", "lay", None, None),
        P("len", "wid", "lay", None, None),
        P("len", "wid", "lay", None),
        P("len", "wid", "lay", None, None),
    )
    out_specs = (P(None, "len", "wid", "lay"), P(None, "len", "wid", "lay"))
    return jax.shard_map(
        per_device, mesh=mesh, in_specs=in_specs, out_specs=out_specs, check_vma=False
    )
```

profile of v0, /device:TPU:0, one launch (start us, length us, event | category | flops | bytes accessed | tf_op | source)
XLA Modules:
  0.0 1301.8 jit_solution(9294549832238594592)
XLA Ops:
  4.6 8.3 all-to-all-start
  13.7 3.8 collective-permute-start.6
  20.8 5.2 collective-permute-start
  29.4 14.1 %gather_fusion.4 = f32[4096,3]{1,0:T(8,128)} fusion(f32[3,4096]{0,1:T(8,128)S(1)} %bitcast.312, s32[4096]{0:T(1024)S(1)} %get-tuple-element.130), kind=kCustom, calls=%fused_computation.6 | custom fusion | bytes 114688 | tf_op jit(solution)/shard_map/gather | solution.py:104
  45.7 14.1 %gather_fusion.3 = f32[4096,3]{1,0:T(8,128)} fusion(f32[3,4096]{0,1:T(8,128)S(1)} %bitcast.313, s32[4096]{0:T(1024)S(1)} %get-tuple-element.129), kind=kCustom, calls=%fused_computation.5 | custom fusion | bytes 114688 | tf_op jit(solution)/shard_map/gather | solution.py:103
  62.1 14.1 %gather_fusion.2 = f32[4096,3]{1,0:T(8,128)} fusion(f32[3,4096]{0,1:T(8,128)S(1)} %bitcast.314, s32[4096]{0:T(1024)S(1)} %get-tuple-element.128), kind=kCustom, calls=%fused_computation.4 | custom fusion | bytes 114688 | tf_op jit(solution)/shard_map/gather | solution.py:102
  78.4 14.1 %gather_fusion.1 = f32[4096,3]{1,0:T(8,128)} fusion(f32[3,4096]{0,1:T(8,128)S(1)} %bitcast.315, s32[4096]{0:T(1024)S(1)} %get-tuple-element.127), kind=kCustom, calls=%fused_computation.3 | custom fusion | bytes 114688 | tf_op jit(solution)/shard_map/gather | solution.py:101
  95.9 27.7 %gather_fusion = f32[8192,3]{1,0:T(8,128)} fusion(f32[3,4096]{0,1:T(8,128)S(1)} %bitcast.316, s32[8192]{0:T(1024)S(1)} %broadcast_clamp_fusion), kind=kCustom, calls=%fused_computation.2 | custom fusion | bytes 229376 | tf_op jit(solution)/shard_map/gather | solution.py:229
  123.6 2.8 copy.205
  129.0 6.1 all-to-all-start.1
  137.2 4.5 collective-permute-start.2
  144.5 3.0 collective-permute-start.4
  148.9 5.4 collective-permute-start.8
  165.8 286.1 %gather_fusion.14 = f32[49152]{0:T(1024)S(1)} fusion(f32[64,6,128]{2,1,0:T(8,128)S(1)} %gather_fusion.6, s32[49152]{0:T(1024)S(1)} %reshape.720), kind=kCustom, calls=%fused_computation.clone | custom fusion | bytes 983040 | tf_op jit(solution)/shard_map/jit(take_along_axis)/gather | solution.py:233
  452.4 2.7 copy.220
  455.1 46.7 %scatter_custom_fusion.2 = f32[3,8192]{0,1:T(8,128)} fusion(s32[8192]{0:T(1024)} %bitcast.365, f32[8192,3]{1,0:T(8,128)} %copy.220, f32[]{:T(128)} %constant.51.clone.1), kind=kCustom, calls=%fused_computation.33 | custom fusion | flops 24576 | bytes 98816 | tf_op jit(solution)/shard_map/scatter-add | solution.py:146
  501.8 2.8 copy.221
  504.7 2.4 scatter_fusion
  507.8 9.5 all-to-all-start.2
  518.5 2.7 copy.218
  521.2 44.8 %scatter_custom_fusion.1 = f32[3,4096]{0,1:T(8,128)S(1)} fusion(s32[8192]{0:T(1024)} %fusion.134, f32[8192,3]{1,0:T(8,128)} %copy.218, f32[]{:T(128)} %constant.51.clone.1), kind=kCustom, calls=%fused_computation.41 | custom fusion | flops 24576 | bytes 49664 | tf_op jit(solution)/shard_map/scatter-add | solution.py:251
  570.0 23.4 %scatter_fusion.1 = f32[3,4096]{0,1:T(8,128)S(1)} fusion(f32[3,4096]{0,1:T(8,128)S(1)} %scatter_custom_fusion.1, s32[4096]{0:T(1024)S(1)} %copy-done.17, f32[4096,3]{1,0:T(8,128)} %bitcast.323), kind=kCustom, calls=%fused_computation.20 | custom fusion | flops 12288 | bytes 163840 | tf_op jit(solution)/shard_map/scatter-add | solution.py:252
  593.4 23.4 %scatter_fusion.2 = f32[3,4096]{0,1:T(8,128)S(1)} fusion(f32[3,4096]{0,1:T(8,128)S(1)} %scatter_fusion.1, s32[4096]{0:T(1024)S(1)} %copy-done.15, f32[4096,3]{1,0:T(8,128)} %bitcast.324), kind=kCustom, calls=%fused_computation.21 | custom fusion | flops 12288 | bytes 163840 | tf_op jit(solution)/shard_map/scatter-add | solution.py:253
  616.9 23.4 %scatter_fusion.3 = f32[3,4096]{0,1:T(8,128)S(1)} fusion(f32[3,4096]{0,1:T(8,128)S(1)} %scatter_fusion.2, s32[4096]{0:T(1024)S(1)} %copy-done.13, f32[4096,3]{1,0:T(8,128)} %bitcast.325), kind=kCustom, calls=%fused_computation.22 | custom fusion | flops 12288 | bytes 163840 | tf_op jit(solution)/shard_map/scatter-add | solution.py:254
  640.4 23.6 %scatter_fusion.4 = f32[3,4096]{0,1:T(8,128)S(1)} fusion(f32[3,4096]{0,1:T(8,128)S(1)} %scatter_fusion.3, s32[4096]{0:T(1024)S(1)} %get-tuple-element.123, f32[4096,3]{1,0:T(8,128)} %bitcast.326), kind=kCustom, calls=%fused_computation.23 | custom fusion | flops 12288 | bytes 163840 | tf_op jit(solution)/shard_map/scatter-add | solution.py:255
  664.7 3.1 multiply_add_fusion.15
  668.6 14.1 %gather_fusion.11 = f32[4096,3]{1,0:T(8,128)} fusion(f32[3,4096]{0,1:T(8,128)S(1)} %bitcast.307, s32[4096]{0:T(1024)S(1)} %copy-done.34), kind=kCustom, calls=%fused_computation.13 | custom fusion | bytes 114688 | tf_op jit(solution)/shard_map/gather | solution.py:104
  682.7 14.1 %gather_fusion.10 = f32[4096,3]{1,0:T(8,128)} fusion(f32[3,4096]{0,1:T(8,128)S(1)} %bitcast.308, s32[4096]{0:T(1024)S(1)} %copy-done.32), kind=kCustom, calls=%fused_computation.12 | custom fusion | bytes 114688 | tf_op jit(solution)/shard_map/gather | solution.py:103
  696.7 14.1 %gather_fusion.9 = f32[4096,3]{1,0:T(8,128)} fusion(f32[3,4096]{0,1:T(8,128)S(1)} %bitcast.309, s32[4096]{0:T(1024)S(1)} %copy-done.30), kind=kCustom, calls=%fused_computation.11 | custom fusion | bytes 114688 | tf_op jit(solution)/shard_map/gather | solution.py:102
  710.8 14.1 %gather_fusion.8 = f32[4096,3]{1,0:T(8,128)} fusion(f32[3,4096]{0,1:T(8,128)S(1)} %bitcast.310, s32[4096]{0:T(1024)S(1)} %copy-done.28), kind=kCustom, calls=%fused_computation.10 | custom fusion | bytes 114688 | tf_op jit(solution)/shard_map/gather | solution.py:101
  735.3 4.5 collective-permute-start.12
  742.6 4.5 collective-permute-start.14
  752.8 27.7 %gather_fusion.7 = f32[8192,3]{1,0:T(8,128)} fusion(f32[3,4096]{0,1:T(8,128)S(1)} %bitcast.311, s32[8192]{0:T(1024)S(1)} %copy-done.7), kind=kCustom, calls=%fused_computation.9 | custom fusion | bytes 229376 | tf_op jit(solution)/shard_map/gather | solution.py:229
  780.5 9.4 all-to-all-start.3
  790.0 2.8 copy.231
  797.7 4.6 all-to-all-done.3
  803.1 286.1 %gather_fusion.15 = f32[49152]{0:T(1024)S(1)} fusion(f32[64,6,128]{2,1,0:T(8,128)S(1)} %gather_fusion.13, s32[49152]{0:T(1024)S(1)} %reshape.720), kind=kCustom, calls=%fused_computation.1.clone | custom fusion | bytes 983040 | tf_op jit(solution)/shard_map/jit(take_along_axis)/gather | solution.py:233
  1089.7 2.7 copy.240
  1092.4 46.5 %scatter_custom_fusion.9 = f32[3,8192]{0,1:T(8,128)} fusion(s32[8192]{0:T(1024)} %bitcast.366, f32[8192,3]{1,0:T(8,128)} %copy.240, f32[]{:T(128)} %constant.51.clone.1), kind=kCustom, calls=%fused_computation.31 | custom fusion | flops 24576 | bytes 98816 | tf_op jit(solution)/shard_map/scatter-add | solution.py:146
  1138.9 2.8 copy.241
  1145.0 5.5 all-to-all-start.4
  1151.5 2.6 copy.239
  1154.2 44.8 %scatter_custom_fusion.8 = f32[3,4096]{0,1:T(8,128)S(1)} fusion(s32[8192]{0:T(1024)} %fusion.134, f32[8192,3]{1,0:T(8,128)} %copy.239, f32[]{:T(128)} %constant.51.clone.1), kind=kCustom, calls=%fused_computation.39 | custom fusion | flops 24576 | bytes 49664 | tf_op jit(solution)/shard_map/scatter-add | solution.py:251
  1203.9 23.4 %scatter_fusion.6 = f32[3,4096]{0,1:T(8,128)S(1)} fusion(f32[3,4096]{0,1:T(8,128)S(1)} %scatter_custom_fusion.8, s32[4096]{0:T(1024)S(1)} %copy-done.18, f32[4096,3]{1,0:T(8,128)} %bitcast.319), kind=kCustom, calls=%fused_computation.27 | custom fusion | flops 12288 | bytes 163840 | tf_op jit(solution)/shard_map/scatter-add | solution.py:252
  1227.4 23.4 %scatter_fusion.7 = f32[3,4096]{0,1:T(8,128)S(1)} fusion(f32[3,4096]{0,1:T(8,128)S(1)} %scatter_fusion.6, s32[4096]{0:T(1024)S(1)} %copy-done.16, f32[4096,3]{1,0:T(8,128)} %bitcast.320), kind=kCustom, calls=%fused_computation.28 | custom fusion | flops 12288 | bytes 163840 | tf_op jit(solution)/shard_map/scatter-add | solution.py:253
  1250.9 23.4 %scatter_fusion.8 = f32[3,4096]{0,1:T(8,128)S(1)} fusion(f32[3,4096]{0,1:T(8,128)S(1)} %scatter_fusion.7, s32[4096]{0:T(1024)S(1)} %copy-done.14, f32[4096,3]{1,0:T(8,128)} %bitcast.321), kind=kCustom, calls=%fused_computation.29 | custom fusion | flops 12288 | bytes 163840 | tf_op jit(solution)/shard_map/scatter-add | solution.py:254
  1274.3 23.4 %scatter_fusion.9 = f32[3,4096]{0,1:T(8,128)S(1)} fusion(f32[3,4096]{0,1:T(8,128)S(1)} %scatter_fusion.8, s32[4096]{0:T(1024)S(1)} %copy-done.12, f32[4096,3]{1,0:T(8,128)} %bitcast.322), kind=kCustom, calls=%fused_computation.30 | custom fusion | flops 12288 | bytes 163840 | tf_op jit(solution)/shard_map/scatter-add | solution.py:255
  1298.4 2.9 multiply_add_fusion.14
  (268 shorter events, 83.4 us)
Async XLA Ops:
  4.6 121.9 %all-to-all-start = ((s32[16,1,8]{2,1,0:T(1,128)}), s32[16,1,8]{2,1,0:T(1,128)S(1)}, u32[]{:S(2)}, u32[]{:S(2)}) async-start(s32[16,1,8]{2,1,0:T(1,128)} %bitcast.40), calls=%async_computation | async-start | bytes 16384 | tf_op jit(solution)/shard_map/all_to_all | solution.py:205
  13.7 128.1 %collective-permute-start.6 = (f32[3,1,8,128]{3,2,1,0:T(8,128)S(1)}, f32[3,1,8,128]{3,2,1,0:T(8,128)S(1)}, u32[]{:S(2)}, u32[]{:S(2)}) collective-permute-start(f32[3,1,8,128]{3,2,1,0:T(8,128)S(1)} %get-tuple-element.120), channel_id=1, source_target_pairs={{0,8},{8,16},{16,24},{1,9},{9,17},{17,25},{2,10},{10,18},{18,26},{... | collective-permute-start | bytes 36872 | tf_op jit(solution)/shard_map/ppermute | solution.py:32
  17.5 124.4 %collective-permute-start.7 = (f32[3,1,8,128]{3,2,1,0:T(8,128)S(1)}, f32[3,1,8,128]{3,2,1,0:T(8,128)S(1)}, u32[]{:S(2)}, u32[]{:S(2)}) collective-permute-start(f32[3,1,8,128]{3,2,1,0:T(8,128)S(1)} %get-tuple-element.119), channel_id=1, source_target_pairs={{8,0},{16,8},{24,16},{9,1},{17,9},{25,17},{10,2},{18,10},{26,18},{... | collective-permute-start | bytes 36872 | tf_op jit(solution)/shard_map/ppermute | solution.py:34
  19.5 116.4 %collective-permute-start.1 = (f32[2,1,8,128]{3,2,1,0:T(8,128)S(1)}, f32[2,1,8,128]{3,2,1,0:T(8,128)S(1)}, u32[]{:S(2)}, u32[]{:S(2)}) collective-permute-start(f32[2,1,8,128]{3,2,1,0:T(8,128)S(1)} %get-tuple-element.122), channel_id=1, source_target_pairs={{8,0},{16,8},{24,16},{9,1},{17,9},{25,17},{10,2},{18,10},{26,18},{... | collective-permute-start | bytes 24584 | tf_op jit(solution)/shard_map/ppermute | solution.py:34
  20.8 115.1 %collective-permute-start = (f32[2,1,8,128]{3,2,1,0:T(8,128)S(1)}, f32[2,1,8,128]{3,2,1,0:T(8,128)S(1)}, u32[]{:S(2)}, u32[]{:S(2)}) collective-permute-start(f32[2,1,8,128]{3,2,1,0:T(8,128)S(1)} %get-tuple-element.121), channel_id=1, source_target_pairs={{0,8},{8,16},{16,24},{1,9},{9,17},{17,25},{2,10},{10,18},{18,26},{... | collective-permute-start | bytes 24584 | tf_op jit(solution)/shard_map/ppermute | solution.py:32
  28.1 67.6 %copy-start.35 = (pred[64,128]{1,0:T(8,128)(4,1)}, pred[64,128]{1,0:T(8,128)(4,1)S(1)}, u32[]{:S(2)}) copy-start(pred[64,128]{1,0:T(8,128)(4,1)S(1)} %broadcast_compare_fusion) | copy-start | bytes 24580
  28.7 67.2 %copy-start.6 = (s32[8192]{0:T(1024)}, s32[8192]{0:T(1024)S(1)}, u32[]{:S(2)}) copy-start(s32[8192]{0:T(1024)S(1)} %broadcast_clamp_fusion) | copy-start | bytes 98308
  28.8 49.6 %copy-start.27 = (s32[4096]{0:T(1024)}, s32[4096]{0:T(1024)S(1)}, u32[]{:S(2)}) copy-start(s32[4096]{0:T(1024)S(1)} %get-tuple-element.127) | copy-start | bytes 49156
  29.4 611.0 %copy-start.11 = (s32[4096]{0:T(1024)}, s32[4096]{0:T(1024)S(1)}, u32[]{:S(2)}) copy-start(s32[4096]{0:T(1024)S(1)} %get-tuple-element.123) | copy-start | bytes 49156
  29.4 135.3 %copy-start.44 = (f32[3,3]{0,1:T(4,128)}, f32[3,3]{0,1:T(4,128)S(1)}, u32[]{:S(2)}) copy-start(f32[3,3]{0,1:T(4,128)S(1)} %fusion.154) | copy-start | bytes 112
  129.0 35.9 %all-to-all-start.1 = ((f32[16,8,6,128]{3,1,2,0:T(8,128)}), f32[16,8,6,128]{3,1,2,0:T(8,128)S(1)}, u32[]{:S(2)}, u32[]{:S(2)}) async-start(f32[16,8,6,128]{3,1,2,0:T(8,128)} %copy_multiply_fusion.1), calls=%async_computation.1 | async-start | bytes 786432 | tf_op jit(solution)/shard_map/all_to_all | solution.py:152
  135.9 5.9 collective-permute-start.3
  137.2 5.9 collective-permute-start.2
  143.2 11.0 collective-permute-start.5
  144.5 9.7 collective-permute-start.4
  147.6 7.1 collective-permute-start.9
  148.9 6.7 collective-permute-start.8
  155.8 3.3 collective-permute-start.10
  157.1 3.3 collective-permute-start.11
  165.8 286.2 %copy-start.36 = (pred[64,128]{1,0:T(8,128)(4,1)S(1)}, pred[64,128]{1,0:T(8,128)(4,1)}, u32[]{:S(2)}) copy-start(pred[64,128]{1,0:T(8,128)(4,1)} %copy-done.35) | copy-start | bytes 24580
  165.8 286.3 %copy-start.39 = (f32[1,1,1,64,128]{4,3,2,1,0:T(8,128)S(1)}, f32[1,1,1,64,128]{4,3,2,1,0:T(8,128)}, u32[]{:S(2)}) copy-start(f32[1,1,1,64,128]{4,3,2,1,0:T(8,128)} %param.23) | copy-start | bytes 98308
  507.8 58.2 %all-to-all-start.2 = ((f32[16,8,3,128]{3,1,2,0:T(8,128)}), f32[16,8,3,128]{3,1,2,0:T(8,128)S(1)}, u32[]{:S(2)}, u32[]{:S(2)}) async-start(f32[16,8,3,128]{3,1,2,0:T(8,128)} %copy.222), calls=%async_computation.2 | async-start | bytes 393216 | tf_op jit(solution)/shard_map/all_to_all | solution.py:156
  568.0 48.9 %copy-start.13 = (s32[4096]{0:T(1024)S(1)}, s32[4096]{0:T(1024)}, u32[]{:S(2)}) copy-start(s32[4096]{0:T(1024)} %get-tuple-element.125) | copy-start | bytes 49156
  616.9 47.8 %copy-start.4 = (f32[3,4,8,128]{3,2,1,0:T(8,128)S(1)}, f32[3,4,8,128]{3,2,1,0:T(8,128)}, u32[]{:S(2)}) copy-start(f32[3,4,8,128]{3,2,1,0:T(8,128)} %param.17) | copy-start | bytes 147460
  616.9 47.8 %copy-start.19 = (f32[4,8,128]{2,1,0:T(8,128)S(1)}, f32[4,8,128]{2,1,0:T(8,128)}, u32[]{:S(2)}) copy-start(f32[4,8,128]{2,1,0:T(8,128)} %get-tuple-element.103) | copy-start | bytes 49156
  616.9 47.8 %copy-start.21 = (f32[4,8,128]{2,1,0:T(8,128)S(1)}, f32[4,8,128]{2,1,0:T(8,128)}, u32[]{:S(2)}) copy-start(f32[4,8,128]{2,1,0:T(8,128)} %get-tuple-element.104) | copy-start | bytes 49156
  616.9 47.8 %copy-start.23 = (f32[4,8,128]{2,1,0:T(8,128)S(1)}, f32[4,8,128]{2,1,0:T(8,128)}, u32[]{:S(2)}) copy-start(f32[4,8,128]{2,1,0:T(8,128)} %get-tuple-element.105) | copy-start | bytes 49156
  616.9 47.8 %copy-start.25 = (f32[4,8,128]{2,1,0:T(8,128)S(1)}, f32[4,8,128]{2,1,0:T(8,128)}, u32[]{:S(2)}) copy-start(f32[4,8,128]{2,1,0:T(8,128)} %get-tuple-element.106) | copy-start | bytes 49156
  667.9 43.0 %copy-start.28 = (s32[4096]{0:T(1024)S(1)}, s32[4096]{0:T(1024)}, u32[]{:S(2)}) copy-start(s32[4096]{0:T(1024)} %copy-done.27) | copy-start | bytes 49156
  733.9 6.1 collective-permute-start.13
  735.3 5.9 collective-permute-start.12
  741.3 6.8 collective-permute-start.15
  742.6 5.9 collective-permute-start.14
  748.6 44.2 %collective-permute-start.16 = (f32[3,6,10,1]{3,2,1,0:T(8,128)S(1)}, f32[3,6,10,1]{3,2,1,0:T(8,128)}, u32[]{:S(2)}, u32[]{:S(2)}) collective-permute-start(f32[3,6,10,1]{3,2,1,0:T(8,128)S(1)} %get-tuple-element.87), channel_id=1, source_target_pairs={{0,1},{2,3},{4,5},{6,7},{8,9},{10,11},{12,13},{14,15},{16,17},{18,... | collective-permute-start | bytes 2168 | tf_op jit(solution)/shard_map/ppermute | solution.py:32
  750.6 42.2 %collective-permute-start.17 = (f32[3,6,10,1]{3,2,1,0:T(8,128)S(1)}, f32[3,6,10,1]{3,2,1,0:T(8,128)}, u32[]{:S(2)}, u32[]{:S(2)}) collective-permute-start(f32[3,6,10,1]{3,2,1,0:T(8,128)S(1)} %get-tuple-element.88), channel_id=1, source_target_pairs={{1,0},{3,2},{5,4},{7,6},{9,8},{11,10},{13,12},{15,14},{17,16},{19,... | collective-permute-start | bytes 2168 | tf_op jit(solution)/shard_map/ppermute | solution.py:34
  780.5 21.7 %all-to-all-start.3 = ((f32[16,8,6,128]{3,1,2,0:T(8,128)}), f32[16,8,6,128]{3,1,2,0:T(8,128)S(1)}, u32[]{:S(2)}, u32[]{:S(2)}) async-start(f32[16,8,6,128]{3,1,2,0:T(8,128)} %copy_multiply_fusion), calls=%async_computation.3 | async-start | bytes 786432 | tf_op jit(solution)/shard_map/all_to_all | solution.py:152
  803.1 286.2 %copy-start.37 = (pred[64,128]{1,0:T(8,128)(4,1)S(1)}, pred[64,128]{1,0:T(8,128)(4,1)}, u32[]{:S(2)}) copy-start(pred[64,128]{1,0:T(8,128)(4,1)} %copy-done.35) | copy-start | bytes 24580
  803.1 286.3 %copy-start.40 = (f32[1,1,1,64,128]{4,3,2,1,0:T(8,128)S(1)}, f32[1,1,1,64,128]{4,3,2,1,0:T(8,128)}, u32[]{:S(2)}) copy-start(f32[1,1,1,64,128]{4,3,2,1,0:T(8,128)} %param.23) | copy-start | bytes 98308
  1145.0 54.0 %all-to-all-start.4 = ((f32[16,8,3,128]{3,1,2,0:T(8,128)}), f32[16,8,3,128]{3,1,2,0:T(8,128)}, u32[]{:S(2)}, u32[]{:S(2)}) async-start(f32[16,8,3,128]{3,1,2,0:T(8,128)} %copy.242), calls=%async_computation.4 | async-start | bytes 393216 | tf_op jit(solution)/shard_map/all_to_all | solution.py:156
  1154.2 46.6 %copy-start.47 = (s32[128]{0:T(128)S(1)}, s32[128]{0:T(128)}, u32[]{:S(2)}) copy-start(s32[128]{0:T(128)} %copy-done.46) | copy-start | bytes 1540
  1154.2 46.6 %copy-start.52 = (pred[128]{0:T(512)(128)(4,1)S(1)}, pred[128]{0:T(512)(128)(4,1)}, u32[]{:S(2)}) copy-start(pred[128]{0:T(512)(128)(4,1)} %ge.49) | copy-start | bytes 388
  1154.2 49.7 %copy-start.18 = (s32[4096]{0:T(1024)S(1)}, s32[4096]{0:T(1024)}, u32[]{:S(2)}) copy-start(s32[4096]{0:T(1024)} %get-tuple-element.124) | copy-start | bytes 49156
  1201.9 48.9 %copy-start.14 = (s32[4096]{0:T(1024)S(1)}, s32[4096]{0:T(1024)}, u32[]{:S(2)}) copy-start(s32[4096]{0:T(1024)} %get-tuple-element.125) | copy-start | bytes 49156
  1203.9 70.4 %copy-start.12 = (s32[4096]{0:T(1024)S(1)}, s32[4096]{0:T(1024)}, u32[]{:S(2)}) copy-start(s32[4096]{0:T(1024)} %copy-done.11) | copy-start | bytes 49156
  1250.8 47.6 %copy-start.10 = (f32[3,4,8,128]{3,2,1,0:T(8,128)S(1)}, f32[3,4,8,128]{3,2,1,0:T(8,128)}, u32[]{:S(2)}) copy-start(f32[3,4,8,128]{3,2,1,0:T(8,128)} %get-tuple-element.15) | copy-start | bytes 147460
  1250.8 47.6 %copy-start.20 = (f32[4,8,128]{2,1,0:T(8,128)S(1)}, f32[4,8,128]{2,1,0:T(8,128)}, u32[]{:S(2)}) copy-start(f32[4,8,128]{2,1,0:T(8,128)} %get-tuple-element.103) | copy-start | bytes 49156
  1250.8 47.6 %copy-start.22 = (f32[4,8,128]{2,1,0:T(8,128)S(1)}, f32[4,8,128]{2,1,0:T(8,128)}, u32[]{:S(2)}) copy-start(f32[4,8,128]{2,1,0:T(8,128)} %get-tuple-element.104) | copy-start | bytes 49156
  1250.8 47.6 %copy-start.24 = (f32[4,8,128]{2,1,0:T(8,128)S(1)}, f32[4,8,128]{2,1,0:T(8,128)}, u32[]{:S(2)}) copy-start(f32[4,8,128]{2,1,0:T(8,128)} %get-tuple-element.105) | copy-start | bytes 49156
  (32 other events, 504.4 us)
where the time goes:
time: 1310 us; the launch traced here: 1300 us
  local copies, waits for them, and re-layouts  805 us (61%)
  other arithmetic  397 us (30%)
  starting transfers between devices  84.9 us (6%)
    gather x5, local copies, waits for them, and re-layouts, per_device(): jnp.take_along_axis(mine, jnp.broadcast_to(chosen[:, None, :], (pairs, 6,...  572 us
    scatter-add x2, other arithmetic, face_sums(): summed = jnp.zeros((3, row_count * face_count), jnp.float32).at[:, flat_i...  93.2 us
    scatter-add x2, other arithmetic, per_device(): jnp.zeros((3, node_count), jnp.float32).at[:, slaves].add(slave_part)  89.6 us
    gather x4, local copies, waits for them, and re-layouts, per_device(): slave_disp = u_flat[:, slaves]  61.1 us
    scatter-add x2, other arithmetic, per_device(): contact = contact.at[:, node_four].add(quarter)  47.1 us
    scatter-add x2, other arithmetic, per_device(): contact = contact.at[:, node_two].add(quarter)  46.9 us
    scatter-add x2, other arithmetic, per_device(): contact = contact.at[:, node_three].add(quarter)  46.9 us
    scatter-add x2, other arithmetic, per_device(): contact = contact.at[:, node_one].add(quarter)  46.9 us
  transfers between devices with their start and end apart: 23, of which 6 were waited for; matrix products, arithmetic and copies ran while one was open for 19% of the time, Pallas kernels for 0%

commit v1 on v0

v1 whole, which is shorter than its diff:
```python
import functools

import jax
import jax.numpy as jnp
from jax import lax
from jax.experimental import pallas as pl
from jax.experimental.pallas import tpu as pltpu
from jax.sharding import PartitionSpec as P

STEPS = 2


penalty = 4.0
hourglass = 0.3
time_step = 0.25
corner_offsets = (
    (0, 0, 0),
    (1, 0, 0),
    (0, 1, 0),
    (1, 1, 0),
    (0, 0, 1),
    (1, 0, 1),
    (0, 1, 1),
    (1, 1, 1),
)
f32 = jnp.float32
bf16 = jnp.bfloat16
CHUNK = 8


def padded_2(cells, sides, width):
    for axis, dim in sides:
        count = lax.axis_size(axis)
        ends = count - 1
        head = lax.slice_in_dim(cells, 0, width, axis=dim)
        tail = lax.slice_in_dim(cells, cells.shape[dim] - width, cells.shape[dim], axis=dim)
        cells = jnp.concatenate(
            [
                lax.ppermute(tail, axis, [(i, (i + 1) % count) for i in range(ends)]),
                cells,
                lax.ppermute(head, axis, [((i + 1) % count, i) for i in range(ends)]),
            ],
            axis=dim,
        )
    return cells


def element_mean(values, counts):
    summed = jnp.zeros(counts, jnp.float32)
    for along_x, along_y, along_z in corner_offsets:
        summed = (
            summed
            + values[
                along_x : along_x + counts[0],
                along_y : along_y + counts[1],
                along_z : along_z + counts[2],
            ]
        )
    return summed * 0.125


def corner_forces(points, lame_elem, shear_elem, counts):
    corners = []
    for along_x, along_y, along_z in corner_offsets:
        corners.append(
            points[
                :,
                along_x : along_x + counts[0],
                along_y : along_y + counts[1],
                along_z : along_z + counts[2],
            ]
        )
    mean_disp = corners[0]
    for corner in corners[1:]:
        mean_disp = mean_disp + corner
    mean_disp = mean_disp * 0.125
    columns = []
    for axis_pos in range(3):
        column = jnp.zeros_like(corners[0])
        for offsets, corner in zip(corner_offsets, corners):
            column = column + (2 * offsets[axis_pos] - 1) * corner
        columns.append(column * 0.25)
    gradient = jnp.stack(columns, axis=1)
    strain_trace = gradient[0, 0] + gradient[1, 1] + gradient[2, 2]
    stress = shear_elem * (gradient + jnp.swapaxes(gradient, 0, 1))
    stress = (
        stress + lame_elem * strain_trace * jnp.eye(3, dtype=jnp.float32)[:, :, None, None, None]
    )
    damping = hourglass * shear_elem
    forces = []
    for offsets, corner in zip(corner_offsets, corners):
        unit_signs = [2 * offsets[0] - 1, 2 * offsets[1] - 1, 2 * offsets[2] - 1]
        traction = (
            unit_signs[0] * stress[:, 0]
            + unit_signs[1] * stress[:, 1]
            + unit_signs[2] * stress[:, 2]
        )
        linear = (
            unit_signs[0] * gradient[:, 0]
            + unit_signs[1] * gradient[:, 1]
            + unit_signs[2] * gradient[:, 2]
        )
        forces.append(-0.25 * traction - damping * (corner - mean_disp - 0.5 * linear))
    return forces


def valid_rows(length, position, pieces):
    element_low = jnp.arange(length + 1, dtype=jnp.int32) + position * length - 1
    return ((element_low >= 0) & (element_low <= pieces * length - 2)).astype(jnp.float32)


def halves(x):
    high = x.astype(bf16)
    return high, (x - high.astype(f32)).astype(bf16)


def hot(rows, depth):
    n = rows[0].shape[1]
    iota = lax.broadcasted_iota(jnp.int32, (depth, n), 0)
    return jnp.concatenate(
        [jnp.where(iota == r, 1.0, 0.0).astype(bf16) for r in rows], axis=1
    )


def pick(table, idx, comps, tall):
    lanes = table.shape[1] // 2
    n = idx.shape[1]
    rows = [idx[j : j + 1, :] for j in range(CHUNK)]
    lane_hot = hot([r % lanes for r in rows], lanes)
    wide = jnp.dot(
        table, jnp.concatenate([lane_hot, lane_hot], axis=0), preferred_element_type=f32
    )
    iota = lax.broadcasted_iota(jnp.int32, (tall, n), 0)
    out = [[] for _ in range(comps)]
    for j in range(CHUNK):
        match = iota == jnp.where(rows[j] < 0, -1, rows[j] // lanes)
        for c in range(comps):
            block = wide[c * tall : (c + 1) * tall, j * n : (j + 1) * n]
            out[c].append(jnp.sum(jnp.where(match, block, 0.0), axis=0, keepdims=True))
    return [jnp.concatenate(o, axis=0) for o in out]


def spread(values, idx, tall, lanes):
    n = idx.shape[1]
    rows = [idx[j : j + 1, :] for j in range(CHUNK)]
    lane_hot = hot([r % lanes for r in rows], lanes)
    iota = lax.broadcasted_iota(jnp.int32, (tall, n), 0)
    match = [iota == jnp.where(r < 0, -1, r // lanes) for r in rows]
    blocks = []
    for v in values:
        for half in halves(v):
            half = half.astype(f32)
            blocks.append(
                jnp.concatenate(
                    [
                        jnp.where(match[j], half[j : j + 1, :], 0.0).astype(bf16)
                        for j in range(CHUNK)
                    ],
                    axis=1,
                )
            )
    return lax.dot_general(
        jnp.concatenate(blocks, axis=0),
        lane_hot,
        (((1,), (1,)), ((), ())),
        preferred_element_type=f32,
    )


def joined(halved, comps, tall):
    return [
        halved[2 * c * tall : (2 * c + 1) * tall] + halved[(2 * c + 1) * tall : (2 * c + 2) * tall]
        for c in range(comps)
    ]


def as_table(blocks):
    both = [halves(b) for b in blocks]
    return jnp.concatenate(
        [
            jnp.concatenate([b[0] for b in both], axis=0),
            jnp.concatenate([b[1] for b in both], axis=0),
        ],
        axis=1,
    )


def exact_dot(a, b):
    return jnp.dot(a, b, precision=lax.Precision.HIGHEST, preferred_element_type=f32)


def flat_block(u, c):
    return jnp.concatenate([u[c, i] for i in range(u.shape[1])], axis=0)


def slave_disp_rows(u_ref, slaves_ref, out_ref):
    u = u_ref[...]
    tall = u.shape[1] * u.shape[2]
    table = as_table([flat_block(u, c) for c in range(3)])

    def body(t, _):
        at = pl.ds(pl.multiple_of(t * CHUNK, CHUNK), CHUNK)
        got = pick(table, slaves_ref[at, :], 3, tall)
        for c in range(3):
            out_ref[c, at, :] = got[c]
        return 0

    lax.fori_loop(0, slaves_ref.shape[0] // CHUNK, body, 0)


def slot_matrix(col, row, capacity, slots):
    pairs = row.shape[1]
    earlier = lax.broadcasted_iota(jnp.int32, (pairs, pairs), 0) < lax.broadcasted_iota(
        jnp.int32, (pairs, pairs), 1
    )
    rank = jnp.sum(jnp.where((col == row) & earlier, 1.0, 0.0), axis=0, keepdims=True)
    slot = row * capacity + rank.astype(jnp.int32)
    return jnp.where(
        lax.broadcasted_iota(jnp.int32, (slots, pairs), 0) == slot, 1.0, 0.0
    ).astype(f32)


def to_groups(rows, groups):
    return rows.reshape(groups, rows.shape[0] // groups, rows.shape[1])


def first_send_kernel(
    capacity,
    u_ref, slaves_ref, gap_ref, chosen_ref, col_ref, row_ref, patch_ref, out_ref, slot_ref, rows_ref
):
    groups, _, chunk, n = out_ref.shape
    slots = groups * chunk
    slave_disp_rows(u_ref, slaves_ref, rows_ref)
    to_slot = slot_matrix(col_ref[...], row_ref[...], capacity, slots)
    slot_ref[...] = to_slot
    face_id = (patch_ref[...] * n + chosen_ref[...] + 1).astype(f32)
    for c in range(3):
        out_ref[:, c] = to_groups(exact_dot(to_slot, rows_ref[c]), groups)
    out_ref[:, 3] = to_groups(exact_dot(to_slot, gap_ref[...]), groups)
    out_ref[:, 4] = to_groups(exact_dot(to_slot, face_id) - 1.0, groups)


def next_send_kernel(u_ref, slaves_ref, slot_ref, out_ref, rows_ref):
    groups = out_ref.shape[0]
    slave_disp_rows(u_ref, slaves_ref, rows_ref)
    for c in range(3):
        out_ref[:, c] = to_groups(exact_dot(slot_ref[...], rows_ref[c]), groups)


def face_nodes_rows(static_ref, faces_ref, nodes_ref):
    faces = faces_ref[...]
    patches, n = faces.shape
    table = jnp.concatenate(
        [(faces // n).astype(f32).astype(bf16), (faces % n).astype(f32).astype(bf16)], axis=0
    )
    table = jnp.concatenate([table, jnp.zeros_like(table)], axis=1)

    def body(t, _):
        face_id = static_ref[t, static_ref.shape[1] - 1].astype(jnp.int32)
        high, low = pick(table, face_id, 2, patches)
        node = high.astype(jnp.int32) * n + low.astype(jnp.int32)
        nodes_ref[t] = jnp.where(face_id < 0, -1, node)
        return 0

    lax.fori_loop(0, static_ref.shape[0], body, 0)


def frames(u):
    span_x, span_y, lanes = u.shape[1:]
    iota_x = lax.broadcasted_iota(jnp.int32, (span_x, span_y, lanes), 0)
    iota_y = lax.broadcasted_iota(jnp.int32, (span_x, span_y, lanes), 1)
    valid = (iota_x < span_x - 1) & (iota_y < span_y - 1)

    def shift_x(v):
        return jnp.concatenate([v[1:], v[:1]], axis=0)

    def shift_y(v):
        return jnp.stack([pltpu.roll(v[i], span_y - 1, 0) for i in range(span_x)])

    one = [u[c] for c in range(3)]
    two = [shift_x(v) for v in one]
    four = [shift_y(v) for v in one]
    three = [shift_x(v) for v in four]
    centroid = [(one[c] + two[c] + three[c] + four[c]) * 0.25 for c in range(3)]
    a = [three[0] - one[0] + 1.0, three[1] - one[1] + 1.0, three[2] - one[2]]
    b = [four[0] - two[0] - 1.0, four[1] - two[1] + 1.0, four[2] - two[2]]
    normal = [
        a[1] * b[2] - a[2] * b[1],
        a[2] * b[0] - a[0] * b[2],
        a[0] * b[1] - a[1] * b[0],
    ]
    square = normal[0] * normal[0] + normal[1] * normal[1] + normal[2] * normal[2]
    usable = valid & (square > 0.0)
    scale = jnp.where(usable, 1.0 / jnp.sqrt(jnp.where(usable, square, 1.0)), 0.0)
    return centroid, [v * scale for v in normal]


def owner_rows(u_ref, recv_ref, gap_ref, gap_at, nodes_ref, force_ref, halved_ref):
    u = u_ref[...]
    span_x, span_y, lanes = u.shape[1:]
    tall = span_x * span_y
    centroid, normal = frames(u)
    table = as_table(
        [jnp.concatenate([v[i] for i in range(span_x)], axis=0) for v in centroid + normal]
    )
    halved_ref[...] = jnp.zeros_like(halved_ref)

    def body(t, _):
        idx = nodes_ref[t]
        got = pick(table, idx, 6, tall)
        gap = gap_ref[t, gap_at]
        for c in range(3):
            gap = gap + (recv_ref[t, c] - got[c]) * got[3 + c]
        push = -penalty * jnp.minimum(gap, 0.0)
        force = [push * got[3 + c] for c in range(3)]
        for c in range(3):
            force_ref[t, c] = force[c]
        halved_ref[...] += spread(force, idx, tall, lanes)
        return 0

    lax.fori_loop(0, recv_ref.shape[0], body, 0)
    total = joined(halved_ref[...], 3, tall)
    out = []
    zero = jnp.zeros((span_y, lanes), f32)
    for c in range(3):
        quarter = [-0.25 * total[c][i * span_y : (i + 1) * span_y] for i in range(span_x)]
        in_x = [(quarter[i] if i < span_x - 1 else zero) + (quarter[i - 1] if i else zero) for i in range(span_x)]
        out.append([v + pltpu.roll(v, 1, 0) for v in in_x])
    return out


def owner_first_kernel(u_ref, recv_ref, faces_ref, force_ref, out_ref, nodes_ref, halved_ref):
    face_nodes_rows(recv_ref, faces_ref, nodes_ref)
    out = owner_rows(u_ref, recv_ref, recv_ref, 3, nodes_ref, force_ref, halved_ref)
    for c in range(3):
        for i in range(len(out[c])):
            out_ref[c, i] = out[c][i]


def owner_next_kernel(u_ref, recv_ref, first_ref, nodes_ref, force_ref, out_ref, halved_ref):
    out = owner_rows(u_ref, recv_ref, first_ref, 3, nodes_ref, force_ref, halved_ref)
    for c in range(3):
        for i in range(len(out[c])):
            out_ref[c, i] = out[c][i]


def slave_kernel(recv_ref, slot_ref, slaves_ref, other_ref, out_ref, rows_ref, halved_ref):
    groups, _, capacity, n = recv_ref.shape
    span_x, span_y, lanes = out_ref.shape[1:]
    tall = span_x * span_y
    for c in range(3):
        rows_ref[c] = lax.dot_general(
            slot_ref[...],
            recv_ref[:, c].reshape(groups * capacity, n),
            (((0,), (0,)), ((), ())),
            precision=lax.Precision.HIGHEST,
            preferred_element_type=f32,
        )
    halved_ref[...] = jnp.zeros_like(halved_ref)

    def body(t, _):
        at = pl.ds(pl.multiple_of(t * CHUNK, CHUNK), CHUNK)
        halved_ref[...] += spread(
            [rows_ref[c, at, :] for c in range(3)], slaves_ref[at, :], tall, lanes
        )
        return 0

    lax.fori_loop(0, slaves_ref.shape[0] // CHUNK, body, 0)
    total = joined(halved_ref[...], 3, tall)
    for c in range(3):
        for i in range(span_x):
            out_ref[c, i] = other_ref[c, i] + total[c][i * span_y : (i + 1) * span_y]


def call(kernel, outs, scratch, *args):
    return pl.pallas_call(
        kernel,
        out_shape=[jax.ShapeDtypeStruct(s, d) for s, d in outs],
        in_specs=[pl.BlockSpec(memory_space=pltpu.VMEM)] * len(args),
        out_specs=[pl.BlockSpec(memory_space=pltpu.VMEM)] * len(outs),
        scratch_shapes=[pltpu.VMEM(s, f32) for s in scratch],
        compiler_params=pltpu.CompilerParams(vmem_limit_bytes=40 * 1024 * 1024),
    )(*args)


def exchange(buffer):
    return lax.all_to_all(buffer, ("len", "wid"), split_axis=0, concat_axis=0, tiled=True)


def per_device(
    displacement,
    velocity,
    lame_first,
    shear_modulus,
    nodal_mass,
    slave_nodes,
    initial_gap,
    candidate,
    pair_owner,
    pair_patch,
    master_faces,
):
    span_x, span_y, span_z = (displacement.shape[1], displacement.shape[2], displacement.shape[3])
    n_len = lax.axis_size("len")
    n_wid = lax.axis_size("wid")
    groups = n_len * n_wid
    pairs = slave_nodes.shape[3]
    face_count = slave_nodes.shape[4]
    patches = master_faces.shape[3]
    capacity = max(2, 2 * pairs // groups)
    slots = groups * capacity
    blocks = slots // CHUNK
    tall = span_x * span_y
    slaves = slave_nodes.reshape(pairs, face_count)
    gaps = initial_gap.reshape(pairs, face_count)
    chosen = candidate.reshape(pairs, face_count)
    faces = master_faces.reshape(patches, face_count)
    col = pair_owner.reshape(pairs, 1)
    row = pair_owner.reshape(1, pairs)
    patch = pair_patch.reshape(pairs, 1)
    stacked = jnp.stack([lame_first, shear_modulus])
    rim = padded_2(stacked, (("len", 1), ("wid", 2), ("lay", 3)), 1)
    counts = (span_x + 1, span_y + 1, span_z + 1)
    mask_x = valid_rows(span_x, lax.axis_index("len"), n_len)
    mask_y = valid_rows(span_y, lax.axis_index("wid"), n_wid)
    mask_z = valid_rows(span_z, lax.axis_index("lay"), lax.axis_size("lay"))
    mask_all = mask_x[:, None, None] * mask_y[None, :, None] * mask_z[None, None, :]
    lame_elem = element_mean(rim[0], counts) * mask_all
    shear_elem = element_mean(rim[1], counts) * mask_all
    block = (3, span_x, span_y, span_z)

    def to_blocks(x):
        comps = x.shape[1]
        if capacity == CHUNK:
            return x
        return (
            x.reshape(blocks, CHUNK // capacity, comps, capacity, face_count)
            .transpose(0, 2, 1, 3, 4)
            .reshape(blocks, comps, CHUNK, face_count)
        )

    def from_blocks(x):
        comps = x.shape[1]
        if capacity == CHUNK:
            return x
        return (
            x.reshape(blocks, comps, CHUNK // capacity, capacity, face_count)
            .transpose(0, 2, 1, 3, 4)
            .reshape(groups, comps, capacity, face_count)
        )

    for step in range(STEPS):
        if step == 0:
            sent, to_slot = call(
                functools.partial(first_send_kernel, capacity),
                [((blocks, 5, CHUNK, face_count), f32), ((slots, pairs), f32)],
                [(3, pairs, face_count)],
                displacement, slaves, gaps, chosen, col, row, patch,
            )
        else:
            (sent,) = call(
                next_send_kernel,
                [((blocks, 3, CHUNK, face_count), f32)],
                [(3, pairs, face_count)],
                displacement, slaves, to_slot,
            )
        arrived = to_blocks(exchange(from_blocks(sent)))
        padded = padded_2(displacement, (("len", 1), ("wid", 2), ("lay", 3)), 1)
        forces = corner_forces(padded, lame_elem, shear_elem, counts)
        internal = jnp.zeros((3, span_x, span_y, span_z), jnp.float32)
        for offsets, force in zip(corner_offsets, forces):
            internal = (
                internal
                + force[
                    :,
                    1 - offsets[0] : 1 - offsets[0] + span_x,
                    1 - offsets[1] : 1 - offsets[1] + span_y,
                    1 - offsets[2] : 1 - offsets[2] + span_z,
                ]
            )
        force_shape = ((blocks, 3, CHUNK, face_count), f32)
        halved = [(6 * tall, span_z)]
        if step == 0:
            first = arrived
            force, reaction, nodes = call(
                owner_first_kernel,
                [force_shape, (block, f32), ((blocks, CHUNK, face_count), jnp.int32)],
                halved, displacement, arrived, faces,
            )
        else:
            force, reaction = call(
                owner_next_kernel, [force_shape, (block, f32)],
                halved, displacement, arrived, first, nodes,
            )
        returned = to_blocks(exchange(from_blocks(force)))
        (contact,) = call(
            slave_kernel, [(block, f32)],
            [(3, pairs, face_count)] + halved, returned, to_slot, slaves, reaction,
        )
        velocity = velocity + time_step * (internal + contact) / nodal_mass[None]
        displacement = displacement + time_step * velocity
    return (displacement, velocity)


def solution(mesh):
    in_specs = (
        P(None, "len", "wid", "lay"),
        P(None, "len", "wid", "lay"),
        P("len", "wid", "lay"),
        P("len", "wid", "lay"),
        P("len", "wid", "lay"),
        P("len", "wid", "lay", None, None),
        P("len", "wid", "lay", None, None),
        P("len", "wid", "lay", None, None),
        P("len", "wid", "lay", None, None),
        P("len", "wid", "lay", None),
        P("len", "wid", "lay", None, None),
    )
    out_specs = (P(None, "len", "wid", "lay"), P(None, "len", "wid", "lay"))
    return jax.shard_map(
        per_device, mesh=mesh, in_specs=in_specs, out_specs=out_specs, check_vma=False
    )
```

time: 1310 us -> 157 us (0.12)
  local copies, waits for them, and re-layouts: 805 us -> 5.09 us
  other arithmetic: 397 us -> 14.9 us
  Pallas kernels: 0 us -> 34.8 us
  waiting for transfers between devices: 9.61 us -> 38.6 us
  starting transfers between devices: 84.9 us -> 61 us
    gather x29 -> x0, local copies, waits for them, and re-layouts: 767 us -> none  [the longest x5 572 us: per_device(): jnp.take_along_axis(mine, jnp.broadcast_to(chosen[:, None, :], (pairs, 6,...]
    scatter-add x12 -> x0, other arithmetic: 370 us -> none  [the longest x2 93.2 us: face_sums(): summed = jnp.zeros((3, row_count * face_count), jnp.float32).at[:, flat_i...]
    pallas_call x0 -> x6, Pallas kernels: none -> 34.8 us  [call(): pl.pallas_call(kernel, out_shape=[jax.ShapeDtypeStruct(s, d) for s, d in...]
    all_to_all x5 -> x4, starting transfers between devices: 38.9 us -> 22.1 us  [exchange(): lax.all_to_all(buffer, ('len', 'wid'), split_axis=0, concat_axis=0, tiled...]
    ppermute x9, waiting for transfers between devices: 1.28 us -> 17.7 us  [padded_2(): lax.ppermute(head, axis, [((i + 1) % count, i) for i in range(ends)])]
    all_to_all x5 -> x4, waiting for transfers between devices: 4.57 us -> 20.7 us  [exchange(): lax.all_to_all(buffer, ('len', 'wid'), split_axis=0, concat_axis=0, tiled...]
    reshape x8 -> x2, local copies, waits for them, and re-layouts: 13.7 us -> 0.19 us  [the longest x1 0.1 us: per_device(): col = pair_owner.reshape(pairs, 1)]
  transfers between devices with their start and end apart: 23 -> 22, of which waited for: 6 -> 10; matrix products, arithmetic and copies ran while one was open for 19% -> 7% of each run, Pallas kernels for 0% -> 4%
where the time goes in v1:
time: 157 us; the launch traced here: 156 us
  starting transfers between devices  61 us (39%)
  waiting for transfers between devices  38.6 us (25%)
  Pallas kernels  34.8 us (22%)
  other arithmetic  14.9 us (9%)
  local copies, waits for them, and re-layouts  5.09 us (3%)
    pallas_call x6, Pallas kernels, call(): pl.pallas_call(kernel, out_shape=[jax.ShapeDtypeStruct(s, d) for s, d in...  34.8 us
    ppermute x9, starting transfers between devices, padded_2(): lax.ppermute(tail, axis, [(i, (i + 1) % count) for i in range(ends)])  27.2 us
    all_to_all x4, starting transfers between devices, exchange(): lax.all_to_all(buffer, ('len', 'wid'), split_axis=0, concat_axis=0, tiled...  22.1 us
    all_to_all x4, waiting for transfers between devices, exchange(): lax.all_to_all(buffer, ('len', 'wid'), split_axis=0, concat_axis=0, tiled...  20.7 us
    ppermute x9, waiting for transfers between devices, padded_2(): lax.ppermute(head, axis, [((i + 1) % count, i) for i in range(ends)])  17.7 us
    ppermute x9, starting transfers between devices, padded_2(): lax.ppermute(head, axis, [((i + 1) % count, i) for i in range(ends)])  11.6 us
    add x2, other arithmetic, per_device(): displacement = displacement + time_step * velocity  4.69 us
    add x4, other arithmetic, corner_forces(): unit_signs[0] * gradient[:, 0] + unit_signs[1] * gradient[:, 1]  4.13 us
  transfers between devices with their start and end apart: 22, of which 10 were waited for; matrix products, arithmetic and copies ran while one was open for 7% of the time, Pallas kernels for 4%

profile of v1, /device:TPU:0, one launch (start us, length us, event | category | flops | bytes accessed | tf_op | source)
XLA Modules:
  0.0 155.7 jit_solution(17560494112600689767)
XLA Ops:
  0.7 0.7 fusion.131
  1.4 4.9 %collective-permute-start.6 = (f32[3,1,8,128]{3,2,1,0:T(8,128)S(1)}, f32[3,1,8,128]{3,2,1,0:T(8,128)S(1)}, u32[]{:S(2)}, u32[]{:S(2)}) collective-permute-start(f32[3,1,8,128]{3,2,1,0:T(8,128)S(1)} %get-tuple-element.109), channel_id=1, source_target_pairs={{0,8},{8,16},{16,24},{1,9},{9,17},{17,25},{2,10},{10,18},{18,26},{... | collective-permute-start | bytes 36872 | tf_op jit(solution)/shard_map/ppermute | solution.py:39
  6.3 1.3 collective-permute-start.7
  7.7 4.7 %collective-permute-start = (f32[2,1,8,128]{3,2,1,0:T(8,128)S(1)}, f32[2,1,8,128]{3,2,1,0:T(8,128)S(1)}, u32[]{:S(2)}, u32[]{:S(2)}) collective-permute-start(f32[2,1,8,128]{3,2,1,0:T(8,128)S(1)} %get-tuple-element.110), channel_id=1, source_target_pairs={{0,8},{8,16},{16,24},{1,9},{9,17},{17,25},{2,10},{10,18},{18,26},{... | collective-permute-start | bytes 24584 | tf_op jit(solution)/shard_map/ppermute | solution.py:39
  12.4 1.3 collective-permute-start.1
  14.5 3.4 %shard_map.122 = (f32[16,5,8,128]{3,2,1,0:T(8,128)}, f32[128,64]{1,0:T(8,128)S(1)}) custom-call(f32[3,4,8,128]{3,2,1,0:T(8,128)S(1)} %copy-done, s32[64,128]{1,0:T(8,128)S(1)} %bitcast.93, f32[64,128]{1,0:T(8,128)S(1)} %bitcast.97, s32[64,128]{1,0:T(8,128)S(1)} %bitcast.98, s32[64,1]{1,0:T(8,128)S(1)} %copy.14.col_ref, s32[1,64]{1,0:T(1,128)S(1)} %bitcast.101, ...), custom_call_target="tpu_custom_call" | custom-call | tf_op jit(solution)/shard_map/pallas_call | solution.py:376
  17.8 7.9 %all-to-all-start = ((f32[16,5,8,128]{3,2,1,0:T(8,128)}), f32[16,5,8,128]{3,2,1,0:T(8,128)S(1)}, u32[]{:S(2)}, u32[]{:S(2)}) async-start(f32[16,5,8,128]{3,2,1,0:T(8,128)} %get-tuple-element.9), calls=%async_computation | async-start | bytes 655360 | tf_op jit(solution)/shard_map/all_to_all | solution.py:387
  26.0 3.8 %collective-permute-start.2 = (f32[2,6,1,128]{3,2,1,0:T(1,128)S(1)}, f32[2,6,1,128]{3,2,1,0:T(1,128)S(1)}, u32[]{:S(2)}, u32[]{:S(2)}) collective-permute-start(f32[2,6,1,128]{3,2,1,0:T(1,128)S(1)} %get-tuple-element.106), channel_id=1, source_target_pairs={{0,2},{2,4},{4,6},{1,3},{3,5},{5,7},{8,10},{10,12},{12,14},{9,11},... | collective-permute-start | bytes 18440 | tf_op jit(solution)/shard_map/ppermute | solution.py:39
  29.8 1.3 collective-permute-start.3
  31.2 4.2 %collective-permute-done.3 = f32[2,6,1,128]{3,2,1,0:T(1,128)S(1)} collective-permute-done((f32[2,6,1,128]{3,2,1,0:T(1,128)S(1)}, f32[2,6,1,128]{3,2,1,0:T(1,128)S(1)}, u32[]{:S(2)}, u32[]{:S(2)}) %collective-permute-start.3) | collective-permute-done | bytes 6176 | tf_op jit(solution)/shard_map/ppermute | solution.py:41
  35.5 1.3 collective-permute-start.4
  36.8 1.3 collective-permute-start.5
  38.1 4.2 %collective-permute-start.8 = (f32[3,6,1,128]{3,2,1,0:T(1,128)S(1)}, f32[3,6,1,128]{3,2,1,0:T(1,128)S(1)}, u32[]{:S(2)}, u32[]{:S(2)}) collective-permute-start(f32[3,6,1,128]{3,2,1,0:T(1,128)S(1)} %get-tuple-element.102), channel_id=1, source_target_pairs={{0,2},{2,4},{4,6},{1,3},{3,5},{5,7},{8,10},{10,12},{12,14},{9,11},... | collective-permute-start | bytes 27656 | tf_op jit(solution)/shard_map/ppermute | solution.py:39
  42.3 1.3 collective-permute-start.9
  44.1 3.8 %collective-permute-done.9 = f32[3,6,1,128]{3,2,1,0:T(1,128)S(1)} collective-permute-done((f32[3,6,1,128]{3,2,1,0:T(1,128)S(1)}, f32[3,6,1,128]{3,2,1,0:T(1,128)S(1)}, u32[]{:S(2)}, u32[]{:S(2)}) %collective-permute-start.9) | collective-permute-done | bytes 9248 | tf_op jit(solution)/shard_map/ppermute | solution.py:41
  48.0 1.6 %collective-permute-start.10 = (f32[3,6,10,1]{3,2,1,0:T(8,128)S(1)}, f32[3,6,10,1]{3,2,1,0:T(8,128)S(1)}, u32[]{:S(2)}, u32[]{:S(2)}) collective-permute-start(f32[3,6,10,1]{3,2,1,0:T(8,128)S(1)} %get-tuple-element.84), channel_id=1, source_target_pairs={{0,1},{2,3},{4,5},{6,7},{8,9},{10,11},{12,13},{14,15},{16,17},{18,... | collective-permute-start | bytes 2168 | tf_op jit(solution)/shard_map/ppermute | solution.py:39
  49.6 1.3 collective-permute-start.11
  51.6 1.3 collective-permute-done.11
  53.1 1.1 broadcast_multiply_fusion.1
  54.3 1.0 multiply_add_fusion.9
  55.3 1.1 multiply_add_fusion.8
  57.3 13.4 %shard_map.123 = (f32[16,3,8,128]{3,2,1,0:T(8,128)}, f32[3,4,8,128]{3,2,1,0:T(8,128)S(1)}, s32[16,8,128]{2,1,0:T(8,128)S(1)}) custom-call(f32[3,4,8,128]{3,2,1,0:T(8,128)S(1)} %copy-done, f32[16,5,8,128]{3,2,1,0:T(8,128)S(1)} %all-to-all-done.recv_ref.first_ref, s32[32,128]{1,0:T(8,128)S(1)} %bitcast.99), custom_call_target="tpu_custom_call" | custom-call | tf_op jit(solution)/shard_map/pallas_call | solution.py:376
  70.7 5.5 %all-to-all-start.1 = ((f32[16,3,8,128]{3,2,1,0:T(8,128)}), f32[16,3,8,128]{3,2,1,0:T(8,128)S(1)}, u32[]{:S(2)}, u32[]{:S(2)}) async-start(f32[16,3,8,128]{3,2,1,0:T(8,128)} %get-tuple-element.10), calls=%async_computation.1 | async-start | bytes 393216 | tf_op jit(solution)/shard_map/all_to_all | solution.py:387
  76.3 1.0 broadcast_multiply_fusion.9
  77.3 7.9 %all-to-all-done.1.recv_ref = f32[16,3,8,128]{3,2,1,0:T(8,128)S(1)} async-done(((f32[16,3,8,128]{3,2,1,0:T(8,128)}), f32[16,3,8,128]{3,2,1,0:T(8,128)S(1)}, u32[]{:S(2)}, u32[]{:S(2)}) %all-to-all-start.1) | async-done | bytes 196640 | tf_op jit(solution)/shard_map/all_to_all | solution.py:387
  85.2 2.8 %shard_map.124 = f32[3,4,8,128]{3,2,1,0:T(8,128)S(1)} custom-call(f32[16,3,8,128]{3,2,1,0:T(8,128)S(1)} %all-to-all-done.1.recv_ref, f32[128,64]{1,0:T(8,128)S(1)} %get-tuple-element.11.slot_ref, s32[64,128]{1,0:T(8,128)S(1)} %bitcast.94, f32[3,4,8,128]{3,2,1,0:T(8,128)S(1)} %get-tuple-element.12.other_ref), custom_call_target="tpu_custom_call" | custom-call | tf_op jit(solution)/shard_map/pallas_call | solution.py:376
  88.7 2.0 %multiply_add_fusion.15 = (f32[3,4,8,128]{3,2,1,0:T(8,128)S(1)}, f32[3,4,8,128]{3,2,1,0:T(8,128)S(1)}) fusion(f32[3,4,8,128]{3,2,1,0:T(8,128)S(1)} %copy-done, f32[3,4,8,128]{3,2,1,0:T(8,128)S(1)} %copy-done.14, f32[4,8,128]{2,1,0:T(8,128)S(1)} %copy-done.12, f32[3,4,8,128]{3,2,1,0:T(8,128)S(1)} %shard_map.124, f32[3,5,9,129]{3,2,1,0:T(8,128)S(1)} %get-tuple-element.112, ...), kind=kLoop, calls=%fused_computation.235 | loop fusion | flops 946176 | bytes 2752512 | tf_op jit(solution)/shard_map/add | solution.py:501
  90.8 2.9 %collective-permute-start.12 = (f32[3,1,8,128]{3,2,1,0:T(8,128)S(1)}, f32[3,1,8,128]{3,2,1,0:T(8,128)S(1)}, u32[]{:S(2)}, u32[]{:S(2)}) collective-permute-start(f32[3,1,8,128]{3,2,1,0:T(8,128)S(1)} %get-tuple-element.104), channel_id=1, source_target_pairs={{0,8},{8,16},{16,24},{1,9},{9,17},{17,25},{2,10},{10,18},{18,26},{... | collective-permute-start | bytes 36872 | tf_op jit(solution)/shard_map/ppermute | solution.py:39
  93.6 1.3 collective-permute-start.13
  95.0 4.2 %collective-permute-done.13 = f32[3,1,8,128]{3,2,1,0:T(8,128)S(1)} collective-permute-done((f32[3,1,8,128]{3,2,1,0:T(8,128)S(1)}, f32[3,1,8,128]{3,2,1,0:T(8,128)S(1)}, u32[]{:S(2)}, u32[]{:S(2)}) %collective-permute-start.13) | collective-permute-done | bytes 12320 | tf_op jit(solution)/shard_map/ppermute | solution.py:41
  99.3 2.5 %collective-permute-start.14 = (f32[3,6,1,128]{3,2,1,0:T(1,128)S(1)}, f32[3,6,1,128]{3,2,1,0:T(1,128)S(1)}, u32[]{:S(2)}, u32[]{:S(2)}) collective-permute-start(f32[3,6,1,128]{3,2,1,0:T(1,128)S(1)} %get-tuple-element.100), channel_id=1, source_target_pairs={{0,2},{2,4},{4,6},{1,3},{3,5},{5,7},{8,10},{10,12},{12,14},{9,11},... | collective-permute-start | bytes 27656 | tf_op jit(solution)/shard_map/ppermute | solution.py:39
  101.7 1.3 collective-permute-start.15
  103.1 4.2 %collective-permute-done.15 = f32[3,6,1,128]{3,2,1,0:T(1,128)S(1)} collective-permute-done((f32[3,6,1,128]{3,2,1,0:T(1,128)S(1)}, f32[3,6,1,128]{3,2,1,0:T(1,128)S(1)}, u32[]{:S(2)}, u32[]{:S(2)}) %collective-permute-start.15) | collective-permute-done | bytes 9248 | tf_op jit(solution)/shard_map/ppermute | solution.py:41
  107.4 1.3 collective-permute-start.16
  108.7 1.3 collective-permute-start.17
  110.0 3.1 %shard_map.125 = f32[16,3,8,128]{3,2,1,0:T(8,128)} custom-call(f32[3,4,8,128]{3,2,1,0:T(8,128)S(1)} %get-tuple-element.23.u_ref, s32[64,128]{1,0:T(8,128)S(1)} %bitcast.95, f32[128,64]{1,0:T(8,128)S(1)} %get-tuple-element.11.slot_ref), custom_call_target="tpu_custom_call" | custom-call | tf_op jit(solution)/shard_map/pallas_call | solution.py:376
  113.2 4.8 %all-to-all-start.2 = ((f32[16,3,8,128]{3,2,1,0:T(8,128)}), f32[16,3,8,128]{3,2,1,0:T(8,128)S(1)}, u32[]{:S(2)}, u32[]{:S(2)}) async-start(f32[16,3,8,128]{3,2,1,0:T(8,128)} %shard_map.125), calls=%async_computation.2 | async-start | bytes 393216 | tf_op jit(solution)/shard_map/all_to_all | solution.py:387
  118.2 1.0 multiply_add_fusion.3
  119.2 1.1 broadcast_multiply_fusion
  120.4 1.0 multiply_add_fusion.2
  122.3 5.1 %all-to-all-done.2.recv_ref = f32[16,3,8,128]{3,2,1,0:T(8,128)S(1)} async-done(((f32[16,3,8,128]{3,2,1,0:T(8,128)}), f32[16,3,8,128]{3,2,1,0:T(8,128)S(1)}, u32[]{:S(2)}, u32[]{:S(2)}) %all-to-all-start.2) | async-done | bytes 196640 | tf_op jit(solution)/shard_map/all_to_all | solution.py:387
  127.4 9.4 %shard_map.126 = (f32[16,3,8,128]{3,2,1,0:T(8,128)}, f32[3,4,8,128]{3,2,1,0:T(8,128)S(1)}) custom-call(f32[3,4,8,128]{3,2,1,0:T(8,128)S(1)} %get-tuple-element.23.u_ref, f32[16,3,8,128]{3,2,1,0:T(8,128)S(1)} %all-to-all-done.2.recv_ref, f32[16,5,8,128]{3,2,1,0:T(8,128)S(1)} %all-to-all-done.recv_ref.first_ref, s32[16,8,128]{2,1,0:T(8,128)S(1)} %get-tuple-element.13.nodes_ref), custom_call_target="tpu_custom_call" | custom-call | tf_op jit(solution)/shard_map/pallas_call | solution.py:376
  136.8 3.9 %all-to-all-start.3 = ((f32[16,3,8,128]{3,2,1,0:T(8,128)}), f32[16,3,8,128]{3,2,1,0:T(8,128)S(1)}, u32[]{:S(2)}, u32[]{:S(2)}) async-start(f32[16,3,8,128]{3,2,1,0:T(8,128)} %get-tuple-element.14), calls=%async_computation.3 | async-start | bytes 393216 | tf_op jit(solution)/shard_map/all_to_all | solution.py:387
  140.7 1.0 broadcast_multiply_fusion.8
  141.8 7.8 %all-to-all-done.3.recv_ref = f32[16,3,8,128]{3,2,1,0:T(8,128)S(1)} async-done(((f32[16,3,8,128]{3,2,1,0:T(8,128)}), f32[16,3,8,128]{3,2,1,0:T(8,128)S(1)}, u32[]{:S(2)}, u32[]{:S(2)}) %all-to-all-start.3) | async-done | bytes 196640 | tf_op jit(solution)/shard_map/all_to_all | solution.py:387
  149.5 2.8 %shard_map.127 = f32[3,4,8,128]{3,2,1,0:T(8,128)S(1)} custom-call(f32[16,3,8,128]{3,2,1,0:T(8,128)S(1)} %all-to-all-done.3.recv_ref, f32[128,64]{1,0:T(8,128)S(1)} %get-tuple-element.11.slot_ref, s32[64,128]{1,0:T(8,128)S(1)} %bitcast.96, f32[3,4,8,128]{3,2,1,0:T(8,128)S(1)} %get-tuple-element.15.other_ref), custom_call_target="tpu_custom_call" | custom-call | tf_op jit(solution)/shard_map/pallas_call | solution.py:376
  152.3 0.7 copy-done.9
  153.0 2.7 %multiply_add_fusion.14 = (f32[3,4,8,128]{3,2,1,0:T(8,128)}, f32[3,4,8,128]{3,2,1,0:T(8,128)}) fusion(f32[3,4,8,128]{3,2,1,0:T(8,128)S(1)} %get-tuple-element.23.u_ref, f32[3,4,8,128]{3,2,1,0:T(8,128)S(1)} %get-tuple-element.24, f32[4,8,128]{2,1,0:T(8,128)S(1)} %copy-done.13, f32[3,4,8,128]{3,2,1,0:T(8,128)S(1)} %shard_map.127, ...), kind=kLoop, calls=%fused_computation.234 | loop fusion | flops 946176 | bytes 2752512 | tf_op jit(solution)/shard_map/add | solution.py:501
  (85 shorter events, 5.6 us)
Async XLA Ops:
  0.6 7.0 %copy-start.7 = (f32[4,8,128]{2,1,0:T(8,128)S(1)}, f32[4,8,128]{2,1,0:T(8,128)}, u32[]{:S(2)}) copy-start(f32[4,8,128]{2,1,0:T(8,128)} %param.13) | copy-start | bytes 49156
  0.6 7.0 %copy-start.6 = (f32[4,8,128]{2,1,0:T(8,128)S(1)}, f32[4,8,128]{2,1,0:T(8,128)}, u32[]{:S(2)}) copy-start(f32[4,8,128]{2,1,0:T(8,128)} %param.14) | copy-start | bytes 49156
  0.7 13.3 %copy-start.3 = (s32[1,1,1,64,128]{4,3,2,1,0:T(8,128)S(1)}, s32[1,1,1,64,128]{4,3,2,1,0:T(8,128)}, u32[]{:S(2)}) copy-start(s32[1,1,1,64,128]{4,3,2,1,0:T(8,128)} %param.18) | copy-start | bytes 98308
  1.4 29.7 %collective-permute-start.6 = (f32[3,1,8,128]{3,2,1,0:T(8,128)S(1)}, f32[3,1,8,128]{3,2,1,0:T(8,128)S(1)}, u32[]{:S(2)}, u32[]{:S(2)}) collective-permute-start(f32[3,1,8,128]{3,2,1,0:T(8,128)S(1)} %get-tuple-element.109), channel_id=1, source_target_pairs={{0,8},{8,16},{16,24},{1,9},{9,17},{17,25},{2,10},{10,18},{18,26},{... | collective-permute-start | bytes 36872 | tf_op jit(solution)/shard_map/ppermute | solution.py:39
  6.3 24.8 %collective-permute-start.7 = (f32[3,1,8,128]{3,2,1,0:T(8,128)S(1)}, f32[3,1,8,128]{3,2,1,0:T(8,128)S(1)}, u32[]{:S(2)}, u32[]{:S(2)}) collective-permute-start(f32[3,1,8,128]{3,2,1,0:T(8,128)S(1)} %get-tuple-element.108), channel_id=1, source_target_pairs={{8,0},{16,8},{24,16},{9,1},{17,9},{25,17},{10,2},{18,10},{26,18},{... | collective-permute-start | bytes 36872 | tf_op jit(solution)/shard_map/ppermute | solution.py:41
  7.6 6.0 %copy-start.5 = (s32[1,1,1,64,1]{3,4,2,1,0:T(1,128)S(1)}, s32[1,1,1,64,1]{3,4,2,1,0:T(1,128)}, u32[]{:S(2)}) copy-start(s32[1,1,1,64,1]{3,4,2,1,0:T(1,128)} %param.19) | copy-start | bytes 772
  7.7 6.2 %copy-start.17 = (s32[1,1,1,64]{3,2,1,0:T(1,128)S(1)}, s32[1,1,1,64]{3,2,1,0:T(1,128)}, u32[]{:S(2)}) copy-start(s32[1,1,1,64]{3,2,1,0:T(1,128)} %param.20) | copy-start | bytes 772
  7.7 6.2 %copy-start.2 = (f32[1,1,1,64,128]{4,3,2,1,0:T(8,128)S(1)}, f32[1,1,1,64,128]{4,3,2,1,0:T(8,128)}, u32[]{:S(2)}) copy-start(f32[1,1,1,64,128]{4,3,2,1,0:T(8,128)} %param.17) | copy-start | bytes 98308
  7.7 6.2 %copy-start = (f32[3,4,8,128]{3,2,1,0:T(8,128)S(1)}, f32[3,4,8,128]{3,2,1,0:T(8,128)}, u32[]{:S(2)}) copy-start(f32[3,4,8,128]{3,2,1,0:T(8,128)} %u_ref.3) | copy-start | bytes 147460
  7.7 18.2 %collective-permute-start = (f32[2,1,8,128]{3,2,1,0:T(8,128)S(1)}, f32[2,1,8,128]{3,2,1,0:T(8,128)S(1)}, u32[]{:S(2)}, u32[]{:S(2)}) collective-permute-start(f32[2,1,8,128]{3,2,1,0:T(8,128)S(1)} %get-tuple-element.110), channel_id=1, source_target_pairs={{0,8},{8,16},{16,24},{1,9},{9,17},{17,25},{2,10},{10,18},{18,26},{... | collective-permute-start | bytes 24584 | tf_op jit(solution)/shard_map/ppermute | solution.py:39
  12.4 13.5 %collective-permute-start.1 = (f32[2,1,8,128]{3,2,1,0:T(8,128)S(1)}, f32[2,1,8,128]{3,2,1,0:T(8,128)S(1)}, u32[]{:S(2)}, u32[]{:S(2)}) collective-permute-start(f32[2,1,8,128]{3,2,1,0:T(8,128)S(1)} %get-tuple-element.111), channel_id=1, source_target_pairs={{8,0},{16,8},{24,16},{9,1},{17,9},{25,17},{10,2},{18,10},{26,18},{... | collective-permute-start | bytes 24584 | tf_op jit(solution)/shard_map/ppermute | solution.py:41
  13.7 0.8 copy-start.1
  17.8 39.0 %all-to-all-start = ((f32[16,5,8,128]{3,2,1,0:T(8,128)}), f32[16,5,8,128]{3,2,1,0:T(8,128)S(1)}, u32[]{:S(2)}, u32[]{:S(2)}) async-start(f32[16,5,8,128]{3,2,1,0:T(8,128)} %get-tuple-element.9), calls=%async_computation | async-start | bytes 655360 | tf_op jit(solution)/shard_map/all_to_all | solution.py:387
  25.8 30.8 %copy-start.15 = (f32[3,3]{0,1:T(4,128)}, f32[3,3]{0,1:T(4,128)S(1)}, u32[]{:S(2)}) copy-start(f32[3,3]{0,1:T(4,128)S(1)} %fusion.114) | copy-start | bytes 112
  26.0 5.2 %collective-permute-start.2 = (f32[2,6,1,128]{3,2,1,0:T(1,128)S(1)}, f32[2,6,1,128]{3,2,1,0:T(1,128)S(1)}, u32[]{:S(2)}, u32[]{:S(2)}) collective-permute-start(f32[2,6,1,128]{3,2,1,0:T(1,128)S(1)} %get-tuple-element.106), channel_id=1, source_target_pairs={{0,2},{2,4},{4,6},{1,3},{3,5},{5,7},{8,10},{10,12},{12,14},{9,11},... | collective-permute-start | bytes 18440 | tf_op jit(solution)/shard_map/ppermute | solution.py:39
  29.8 5.6 %collective-permute-start.3 = (f32[2,6,1,128]{3,2,1,0:T(1,128)S(1)}, f32[2,6,1,128]{3,2,1,0:T(1,128)S(1)}, u32[]{:S(2)}, u32[]{:S(2)}) collective-permute-start(f32[2,6,1,128]{3,2,1,0:T(1,128)S(1)} %get-tuple-element.107), channel_id=1, source_target_pairs={{2,0},{4,2},{6,4},{3,1},{5,3},{7,5},{10,8},{12,10},{14,12},{11,9},... | collective-permute-start | bytes 18440 | tf_op jit(solution)/shard_map/ppermute | solution.py:41
  35.5 8.2 %collective-permute-start.4 = (f32[2,6,10,1]{3,2,1,0:T(8,128)S(1)}, f32[2,6,10,1]{3,2,1,0:T(8,128)S(1)}, u32[]{:S(2)}, u32[]{:S(2)}) collective-permute-start(f32[2,6,10,1]{3,2,1,0:T(8,128)S(1)} %get-tuple-element.86), channel_id=1, source_target_pairs={{0,1},{2,3},{4,5},{6,7},{8,9},{10,11},{12,13},{14,15},{16,17},{18,... | collective-permute-start | bytes 1448 | tf_op jit(solution)/shard_map/ppermute | solution.py:39
  36.8 6.9 %collective-permute-start.5 = (f32[2,6,10,1]{3,2,1,0:T(8,128)S(1)}, f32[2,6,10,1]{3,2,1,0:T(8,128)S(1)}, u32[]{:S(2)}, u32[]{:S(2)}) collective-permute-start(f32[2,6,10,1]{3,2,1,0:T(8,128)S(1)} %get-tuple-element.87), channel_id=1, source_target_pairs={{1,0},{3,2},{5,4},{7,6},{9,8},{11,10},{13,12},{15,14},{17,16},{19,... | collective-permute-start | bytes 1448 | tf_op jit(solution)/shard_map/ppermute | solution.py:41
  38.1 6.0 %collective-permute-start.8 = (f32[3,6,1,128]{3,2,1,0:T(1,128)S(1)}, f32[3,6,1,128]{3,2,1,0:T(1,128)S(1)}, u32[]{:S(2)}, u32[]{:S(2)}) collective-permute-start(f32[3,6,1,128]{3,2,1,0:T(1,128)S(1)} %get-tuple-element.102), channel_id=1, source_target_pairs={{0,2},{2,4},{4,6},{1,3},{3,5},{5,7},{8,10},{10,12},{12,14},{9,11},... | collective-permute-start | bytes 27656 | tf_op jit(solution)/shard_map/ppermute | solution.py:39
  42.3 5.6 %collective-permute-start.9 = (f32[3,6,1,128]{3,2,1,0:T(1,128)S(1)}, f32[3,6,1,128]{3,2,1,0:T(1,128)S(1)}, u32[]{:S(2)}, u32[]{:S(2)}) collective-permute-start(f32[3,6,1,128]{3,2,1,0:T(1,128)S(1)} %get-tuple-element.103), channel_id=1, source_target_pairs={{2,0},{4,2},{6,4},{3,1},{5,3},{7,5},{10,8},{12,10},{14,12},{11,9},... | collective-permute-start | bytes 27656 | tf_op jit(solution)/shard_map/ppermute | solution.py:41
  48.0 3.6 %collective-permute-start.10 = (f32[3,6,10,1]{3,2,1,0:T(8,128)S(1)}, f32[3,6,10,1]{3,2,1,0:T(8,128)S(1)}, u32[]{:S(2)}, u32[]{:S(2)}) collective-permute-start(f32[3,6,10,1]{3,2,1,0:T(8,128)S(1)} %get-tuple-element.84), channel_id=1, source_target_pairs={{0,1},{2,3},{4,5},{6,7},{8,9},{10,11},{12,13},{14,15},{16,17},{18,... | collective-permute-start | bytes 2168 | tf_op jit(solution)/shard_map/ppermute | solution.py:39
  49.6 3.3 %collective-permute-start.11 = (f32[3,6,10,1]{3,2,1,0:T(8,128)S(1)}, f32[3,6,10,1]{3,2,1,0:T(8,128)S(1)}, u32[]{:S(2)}, u32[]{:S(2)}) collective-permute-start(f32[3,6,10,1]{3,2,1,0:T(8,128)S(1)} %get-tuple-element.85), channel_id=1, source_target_pairs={{1,0},{3,2},{5,4},{7,6},{9,8},{11,10},{13,12},{15,14},{17,16},{19,... | collective-permute-start | bytes 2168 | tf_op jit(solution)/shard_map/ppermute | solution.py:41
  56.6 0.7 copy-start.4
  70.7 14.5 %all-to-all-start.1 = ((f32[16,3,8,128]{3,2,1,0:T(8,128)}), f32[16,3,8,128]{3,2,1,0:T(8,128)S(1)}, u32[]{:S(2)}, u32[]{:S(2)}) async-start(f32[16,3,8,128]{3,2,1,0:T(8,128)} %get-tuple-element.10), calls=%async_computation.1 | async-start | bytes 393216 | tf_op jit(solution)/shard_map/all_to_all | solution.py:387
  85.2 2.8 %copy-start.14 = (f32[3,4,8,128]{3,2,1,0:T(8,128)S(1)}, f32[3,4,8,128]{3,2,1,0:T(8,128)}, u32[]{:S(2)}) copy-start(f32[3,4,8,128]{3,2,1,0:T(8,128)} %param.12) | copy-start | bytes 147460
  88.0 0.7 copy-start.12
  88.0 0.7 copy-start.8
  88.0 0.7 copy-start.10
  90.8 4.3 %collective-permute-start.12 = (f32[3,1,8,128]{3,2,1,0:T(8,128)S(1)}, f32[3,1,8,128]{3,2,1,0:T(8,128)S(1)}, u32[]{:S(2)}, u32[]{:S(2)}) collective-permute-start(f32[3,1,8,128]{3,2,1,0:T(8,128)S(1)} %get-tuple-element.104), channel_id=1, source_target_pairs={{0,8},{8,16},{16,24},{1,9},{9,17},{17,25},{2,10},{10,18},{18,26},{... | collective-permute-start | bytes 36872 | tf_op jit(solution)/shard_map/ppermute | solution.py:39
  93.6 5.6 %collective-permute-start.13 = (f32[3,1,8,128]{3,2,1,0:T(8,128)S(1)}, f32[3,1,8,128]{3,2,1,0:T(8,128)S(1)}, u32[]{:S(2)}, u32[]{:S(2)}) collective-permute-start(f32[3,1,8,128]{3,2,1,0:T(8,128)S(1)} %get-tuple-element.105), channel_id=1, source_target_pairs={{8,0},{16,8},{24,16},{9,1},{17,9},{25,17},{10,2},{18,10},{26,18},{... | collective-permute-start | bytes 36872 | tf_op jit(solution)/shard_map/ppermute | solution.py:41
  99.3 3.8 %collective-permute-start.14 = (f32[3,6,1,128]{3,2,1,0:T(1,128)S(1)}, f32[3,6,1,128]{3,2,1,0:T(1,128)S(1)}, u32[]{:S(2)}, u32[]{:S(2)}) collective-permute-start(f32[3,6,1,128]{3,2,1,0:T(1,128)S(1)} %get-tuple-element.100), channel_id=1, source_target_pairs={{0,2},{2,4},{4,6},{1,3},{3,5},{5,7},{8,10},{10,12},{12,14},{9,11},... | collective-permute-start | bytes 27656 | tf_op jit(solution)/shard_map/ppermute | solution.py:39
  101.7 5.6 %collective-permute-start.15 = (f32[3,6,1,128]{3,2,1,0:T(1,128)S(1)}, f32[3,6,1,128]{3,2,1,0:T(1,128)S(1)}, u32[]{:S(2)}, u32[]{:S(2)}) collective-permute-start(f32[3,6,1,128]{3,2,1,0:T(1,128)S(1)} %get-tuple-element.101), channel_id=1, source_target_pairs={{2,0},{4,2},{6,4},{3,1},{5,3},{7,5},{10,8},{12,10},{14,12},{11,9},... | collective-permute-start | bytes 27656 | tf_op jit(solution)/shard_map/ppermute | solution.py:41
  107.4 10.5 %collective-permute-start.16 = (f32[3,6,10,1]{3,2,1,0:T(8,128)S(1)}, f32[3,6,10,1]{3,2,1,0:T(8,128)S(1)}, u32[]{:S(2)}, u32[]{:S(2)}) collective-permute-start(f32[3,6,10,1]{3,2,1,0:T(8,128)S(1)} %get-tuple-element.82), channel_id=1, source_target_pairs={{0,1},{2,3},{4,5},{6,7},{8,9},{10,11},{12,13},{14,15},{16,17},{18,... | collective-permute-start | bytes 2168 | tf_op jit(solution)/shard_map/ppermute | solution.py:39
  108.7 9.2 %collective-permute-start.17 = (f32[3,6,10,1]{3,2,1,0:T(8,128)S(1)}, f32[3,6,10,1]{3,2,1,0:T(8,128)S(1)}, u32[]{:S(2)}, u32[]{:S(2)}) collective-permute-start(f32[3,6,10,1]{3,2,1,0:T(8,128)S(1)} %get-tuple-element.83), channel_id=1, source_target_pairs={{1,0},{3,2},{5,4},{7,6},{9,8},{11,10},{13,12},{15,14},{17,16},{19,... | collective-permute-start | bytes 2168 | tf_op jit(solution)/shard_map/ppermute | solution.py:41
  113.2 14.2 %all-to-all-start.2 = ((f32[16,3,8,128]{3,2,1,0:T(8,128)}), f32[16,3,8,128]{3,2,1,0:T(8,128)S(1)}, u32[]{:S(2)}, u32[]{:S(2)}) async-start(f32[16,3,8,128]{3,2,1,0:T(8,128)} %shard_map.125), calls=%async_computation.2 | async-start | bytes 393216 | tf_op jit(solution)/shard_map/all_to_all | solution.py:387
  121.4 0.7 copy-start.16
  136.8 12.7 %all-to-all-start.3 = ((f32[16,3,8,128]{3,2,1,0:T(8,128)}), f32[16,3,8,128]{3,2,1,0:T(8,128)S(1)}, u32[]{:S(2)}, u32[]{:S(2)}) async-start(f32[16,3,8,128]{3,2,1,0:T(8,128)} %get-tuple-element.14), calls=%async_computation.3 | async-start | bytes 393216 | tf_op jit(solution)/shard_map/all_to_all | solution.py:387
  149.5 2.8 %copy-start.13 = (f32[4,8,128]{2,1,0:T(8,128)S(1)}, f32[4,8,128]{2,1,0:T(8,128)}, u32[]{:S(2)}) copy-start(f32[4,8,128]{2,1,0:T(8,128)} %param.15) | copy-start | bytes 49156
  152.3 0.7 copy-start.9
  152.3 0.7 copy-start.11

commit v2 on v0

v2 whole, which is shorter than its diff:
```python
import functools

import jax
import jax.numpy as jnp
from jax import lax
from jax.experimental import pallas as pl
from jax.experimental.pallas import tpu as pltpu
from jax.sharding import PartitionSpec as P

STEPS = 2


penalty = 4.0
hourglass = 0.3
time_step = 0.25
f32 = jnp.float32
bf16 = jnp.bfloat16
CHUNK = 8
MESH = pl.DeviceIdType.MESH


def halves(x):
    high = x.astype(bf16)
    return high, (x - high.astype(f32)).astype(bf16)


def hots(idx, lanes, tall):
    n = idx.shape[1]
    lane = jnp.where(idx < 0, 0, idx % lanes)
    row = jnp.where(idx < 0, -1, idx // lanes)
    lane_iota = lax.broadcasted_iota(jnp.int32, (lanes, n), 0)
    row_iota = lax.broadcasted_iota(jnp.int32, (tall, n), 0)
    lane_hot = jnp.concatenate(
        [jnp.where(lane_iota == lane[j : j + 1, :], 1.0, 0.0).astype(bf16) for j in range(CHUNK)],
        axis=1,
    )
    return lane_hot, [row_iota == row[j : j + 1, :] for j in range(CHUNK)]


def pick(table, lane_hot, match, comps):
    tall, n = match[0].shape
    wide = jnp.dot(
        table, jnp.concatenate([lane_hot, lane_hot], axis=0), preferred_element_type=f32
    )
    out = []
    for c in range(comps):
        rows = []
        for j in range(CHUNK):
            block = wide[c * tall : (c + 1) * tall, j * n : (j + 1) * n]
            rows.append(jnp.sum(jnp.where(match[j], block, 0.0), axis=0, keepdims=True))
        out.append(jnp.concatenate(rows, axis=0))
    return out


def spread(values, lane_hot, match):
    blocks = []
    for v in values:
        for half in halves(v):
            half = half.astype(f32)
            blocks.append(
                jnp.concatenate(
                    [
                        jnp.where(match[j], half[j : j + 1, :], 0.0).astype(bf16)
                        for j in range(CHUNK)
                    ],
                    axis=1,
                )
            )
    return lax.dot_general(
        jnp.concatenate(blocks, axis=0),
        lane_hot,
        (((1,), (1,)), ((), ())),
        preferred_element_type=f32,
    )


def joined(halved, comps, tall):
    return [
        halved[2 * c * tall : (2 * c + 1) * tall] + halved[(2 * c + 1) * tall : (2 * c + 2) * tall]
        for c in range(comps)
    ]


def as_table(blocks):
    both = [halves(b) for b in blocks]
    return jnp.concatenate(
        [
            jnp.concatenate([b[0] for b in both], axis=0),
            jnp.concatenate([b[1] for b in both], axis=0),
        ],
        axis=1,
    )


def exact_dot(a, b):
    return jnp.dot(a, b, precision=lax.Precision.HIGHEST, preferred_element_type=f32)


def flat_block(u, c):
    return jnp.concatenate([u[c, i] for i in range(u.shape[1])], axis=0)


def slot_matrix(col, row, capacity, slots):
    pairs = row.shape[1]
    earlier = lax.broadcasted_iota(jnp.int32, (pairs, pairs), 0) < lax.broadcasted_iota(
        jnp.int32, (pairs, pairs), 1
    )
    rank = jnp.sum(jnp.where((col == row) & earlier, 1.0, 0.0), axis=0, keepdims=True)
    slot = row * capacity + rank.astype(jnp.int32)
    return jnp.where(
        lax.broadcasted_iota(jnp.int32, (slots, pairs), 0) == slot, 1.0, 0.0
    ).astype(f32)


def frames(u):
    span_x, span_y, lanes = u.shape[1:]
    iota_x = lax.broadcasted_iota(jnp.int32, (span_x, span_y, lanes), 0)
    iota_y = lax.broadcasted_iota(jnp.int32, (span_x, span_y, lanes), 1)
    valid = (iota_x < span_x - 1) & (iota_y < span_y - 1)

    def shift_x(v):
        return jnp.concatenate([v[1:], v[:1]], axis=0)

    def shift_y(v):
        return jnp.stack([pltpu.roll(v[i], span_y - 1, 0) for i in range(span_x)])

    one = [u[c] for c in range(3)]
    two = [shift_x(v) for v in one]
    four = [shift_y(v) for v in one]
    three = [shift_x(v) for v in four]
    centroid = [(one[c] + two[c] + three[c] + four[c]) * 0.25 for c in range(3)]
    a = [three[0] - one[0] + 1.0, three[1] - one[1] + 1.0, three[2] - one[2]]
    b = [four[0] - two[0] - 1.0, four[1] - two[1] + 1.0, four[2] - two[2]]
    normal = [
        a[1] * b[2] - a[2] * b[1],
        a[2] * b[0] - a[0] * b[2],
        a[0] * b[1] - a[1] * b[0],
    ]
    square = normal[0] * normal[0] + normal[1] * normal[1] + normal[2] * normal[2]
    usable = valid & (square > 0.0)
    scale = jnp.where(usable, 1.0 / jnp.sqrt(jnp.where(usable, square, 1.0)), 0.0)
    return centroid, [v * scale for v in normal]


def axis_low(shape, dim, span, start, total):
    iota = lax.broadcasted_iota(jnp.int32, shape, dim)
    size = shape[dim]
    low = jnp.where(iota == size - 1, -1, iota)
    inside = (iota < span) | (iota == size - 1)
    return inside & (low + start >= 0) & (low + start <= total - 2)


def next_z(v):
    return pltpu.roll(v, v.shape[1] - 1, 1)


def next_y(v):
    return pltpu.roll(v, v.shape[0] - 1, 0)


def plane_modes(plane):
    ahead = next_z(plane)
    total, diff = ahead + plane, ahead - plane
    total_y, diff_y = next_y(total), next_y(diff)
    return total_y + total, total_y - total, diff_y + diff, diff_y - diff


def fused_kernel(
    sizes,
    u_ref, v_ref, lame_ref, shear_ref, mass_ref, slaves_ref, gap_ref, chosen_ref, col_ref, row_ref,
    patch_ref, faces_ref,
    uo_ref, vo_ref,
    ring, z_in, y_out, y_in, elem, slot_ref, rows_ref, nodes_ref, halved_ref, inner_ref,
    out_1, out_2, in_1, in_2, force_1, force_2, back_1, back_2,
    go_send, go_recv, back_send, back_recv, halo_send, halo_recv,
):
    n_len, n_wid, n_lay = sizes
    groups = n_len * n_wid
    span_x, span_y, span_z = u_ref.shape[1:]
    tall = span_x * span_y
    capacity, n = out_1.shape[2:]
    slots = groups * capacity
    per = CHUNK // capacity
    pairs = slaves_ref.shape[0]
    patches = faces_ref.shape[0]
    ring_y, ring_z = ring.shape[3:]
    at_len, at_wid, at_lay = lax.axis_index("len"), lax.axis_index("wid"), lax.axis_index("lay")
    me = at_len * n_wid + at_wid

    def peer_id(g):
        return (g // n_wid, g % n_wid, at_lay)

    zero_plane = jnp.zeros((ring_y, ring_z), f32)
    for s in range(STEPS):
        for c in range(5 if s == 0 else 3):
            for i in (span_x, span_x + 1):
                ring[s, c, i] = zero_plane

    barrier = pltpu.get_barrier_semaphore()

    def greet(o, _):
        pl.semaphore_signal(
            barrier, inc=1, device_id=peer_id((me + o) % groups), device_id_type=MESH
        )
        return 0

    lax.fori_loop(1, groups, greet, 0)
    lay_peers = [(at_lay + step) % n_lay for step in sorted({1 % n_lay, (n_lay - 1) % n_lay} - {0})]
    for other in lay_peers:
        pl.semaphore_signal(barrier, inc=1, device_id=(at_len, at_wid, other), device_id_type=MESH)
    pl.semaphore_wait(barrier, groups - 1 + len(lay_peers))

    def halo_copy(s, phase, side):
        comps = pl.ds(0, 5 if s == 0 else 3)
        step = 1 if side == 0 else -1
        place = [at_len, at_wid, at_lay]
        axis = 2 - phase
        count = (n_len, n_wid, n_lay)[axis]
        place[axis] = place[axis] + step
        has = (place[axis] >= 0) & (place[axis] < count)
        if phase == 0:
            src = ring.at[s, comps, pl.ds(0, span_x), pl.ds(0, span_y), pl.ds(0, span_z)]
            dst = z_in.at[s, side, comps]
        elif phase == 1:
            src = y_out.at[s, side, comps]
            dst = y_in.at[s, side, comps]
        else:
            src = ring.at[s, comps, span_x - 1 if side == 0 else 0]
            dst = ring.at[s, comps, span_x + 1 if side == 0 else span_x]
        came = [at_len, at_wid, at_lay][axis] - step
        comes = (came >= 0) & (came < count)
        copy = pltpu.make_async_remote_copy(
            src_ref=src,
            dst_ref=dst,
            send_sem=halo_send.at[s, phase, side],
            recv_sem=halo_recv.at[s, phase, side],
            device_id=tuple(place),
            device_id_type=MESH,
        )
        return copy, has, comes

    def halo_start(s, phase):
        for side in range(2):
            copy, has, _ = halo_copy(s, phase, side)

            @pl.when(has)
            def _():
                copy.start()

    def halo_wait(s, phase):
        for side in range(2):
            copy, _, comes = halo_copy(s, phase, side)

            @pl.when(comes)
            def _():
                copy.wait_recv()

    def halo_sent(s):
        for phase in range(3):
            for side in range(2):
                copy, has, _ = halo_copy(s, phase, side)

                @pl.when(has)
                def _():
                    copy.wait_send()

    def go_copy(s, g, slot):
        return pltpu.make_async_remote_copy(
            src_ref=(out_1, out_2)[s].at[g],
            dst_ref=(in_1, in_2)[s].at[slot],
            send_sem=go_send.at[s, g],
            recv_sem=go_recv.at[s, slot],
            device_id=peer_id(g),
            device_id_type=MESH,
        )

    def back_copy(s, g, slot):
        return pltpu.make_async_remote_copy(
            src_ref=(force_1, force_2)[s].at[g],
            dst_ref=(back_1, back_2)[s].at[slot],
            send_sem=back_send.at[s, g],
            recv_sem=back_recv.at[s, slot],
            device_id=peer_id(g),
            device_id_type=MESH,
        )

    def to_groups(rows):
        return rows.reshape(groups, capacity, n)

    def held(ref, b, c):
        return jnp.concatenate([ref[b * per + k, c] for k in range(per)], axis=0)

    faces = faces_ref[...]
    face_table = jnp.concatenate(
        [(faces // n).astype(f32).astype(bf16), (faces % n).astype(f32).astype(bf16)], axis=0
    )
    face_table = jnp.concatenate([face_table, jnp.zeros_like(face_table)], axis=1)
    lanes_z = lax.broadcasted_iota(jnp.int32, (span_y, span_z), 1)
    rows_y = lax.broadcasted_iota(jnp.int32, (ring_y - span_y, ring_z), 0)

    for s in range(STEPS):
        comps = 5 if s == 0 else 3
        now_u, now_v = (u_ref, v_ref) if s == 0 else (uo_ref, vo_ref)
        out, into, force_ref, back = (
            (out_1, in_1, force_1, back_1) if s == 0 else (out_2, in_2, force_2, back_2)
        )
        for c in range(comps):
            for i in range(span_x):
                ring[s, c, i, 0:span_y, 0:span_z] = (
                    now_u[c, i] if c < 3 else (lame_ref, shear_ref)[c - 3][i]
                )
        halo_start(s, 0)

        u = now_u[...]
        table = as_table([flat_block(u, c) for c in range(3)])

        def gather_rows(t, _):
            at = pl.ds(pl.multiple_of(t * CHUNK, CHUNK), CHUNK)
            got = pick(table, *hots(slaves_ref[at, :], span_z, tall), 3)
            for c in range(3):
                rows_ref[c, at, :] = got[c]
            return 0

        lax.fori_loop(0, pairs // CHUNK, gather_rows, 0)
        if s == 0:
            slot_ref[...] = slot_matrix(col_ref[...], row_ref[...], capacity, slots)
            face_id = (patch_ref[...] * n + chosen_ref[...] + 1).astype(f32)
            out[:, 3] = to_groups(exact_dot(slot_ref[...], gap_ref[...]))
            out[:, 4] = to_groups(exact_dot(slot_ref[...], face_id) - 1.0)
        for c in range(3):
            out[:, c] = to_groups(exact_dot(slot_ref[...], rows_ref[c]))
        into[me] = out[me]

        def send_go(o, _):
            go_copy(s, (me + o) % groups, me).start()
            return 0

        lax.fori_loop(1, groups, send_go, 0)

        halo_wait(s, 0)
        for c in range(comps):
            for i in range(span_x):
                tile = jnp.where((lanes_z == 0) & (at_lay + 1 < n_lay), z_in[s, 1, c, i], 0.0)
                tile = jnp.where((lanes_z == span_z - 1) & (at_lay > 0), z_in[s, 0, c, i], tile)
                ring[s, c, i, 0:span_y, span_z:ring_z] = tile
        for c in range(comps):
            for i in range(span_x):
                y_out[s, 0, c, i : i + 1, :] = ring[s, c, i, span_y - 1 : span_y, :]
                y_out[s, 1, c, i : i + 1, :] = ring[s, c, i, 0:1, :]
        halo_start(s, 1)

        centroid, normal = frames(u)
        frame_table = as_table(
            [jnp.concatenate([v[i] for i in range(span_x)], axis=0) for v in centroid + normal]
        )
        halved_ref[...] = jnp.zeros_like(halved_ref)

        halo_wait(s, 1)
        for c in range(comps):
            for i in range(span_x):
                tile = jnp.where(
                    (rows_y == 0) & (at_wid + 1 < n_wid), y_in[s, 1, c, i : i + 1, :], 0.0
                )
                tile = jnp.where(
                    (rows_y == ring_y - span_y - 1) & (at_wid > 0), y_in[s, 0, c, i : i + 1, :], tile
                )
                ring[s, c, i, span_y:ring_y, :] = tile
        halo_start(s, 2)

        def own(t, _):
            b = (me // per - t + groups // per) % (groups // per)
            for k in range(per):
                g = b * per + k

                @pl.when(g != me)
                def _():
                    go_copy(s, g, g).wait_recv()

            if s == 0:
                face_id = held(in_1, b, 4).astype(jnp.int32)
                high, low = pick(face_table, *hots(face_id, n, patches), 2)
                node = high.astype(jnp.int32) * span_z + low.astype(jnp.int32)
                nodes_ref[b] = jnp.where(face_id < 0, -1, node)
            lane_hot, match = hots(nodes_ref[b], span_z, tall)
            got = pick(frame_table, lane_hot, match, 6)
            gap = held(in_1, b, 3)
            for c in range(3):
                gap = gap + (held(into, b, c) - got[c]) * got[3 + c]
            push = -penalty * jnp.minimum(gap, 0.0)
            force = [push * got[3 + c] for c in range(3)]
            for c in range(3):
                for k in range(per):
                    force_ref[b * per + k, c] = force[c][k * capacity : (k + 1) * capacity]
            for k in range(per):
                g = b * per + k

                @pl.when(g != me)
                def _():
                    back_copy(s, g, me).start()

            halved_ref[...] += spread(force, lane_hot, match)
            return 0

        lax.fori_loop(0, groups // per, own, 0)
        back[me] = force_ref[me]

        total = joined(halved_ref[...], 3, tall)
        zero = jnp.zeros((span_y, span_z), f32)
        for c in range(3):
            quarter = [-0.25 * total[c][i * span_y : (i + 1) * span_y] for i in range(span_x)]
            for i in range(span_x):
                both = (quarter[i] if i < span_x - 1 else zero) + (quarter[i - 1] if i else zero)
                inner_ref[c, i] = both + pltpu.roll(both, 1, 0)

        halo_wait(s, 2)
        planes = [span_x + 1] + list(range(span_x + 1))
        if s == 0:
            shape = (ring_y, ring_z)
            valid = axis_low(shape, 0, span_y, at_wid * span_y, n_wid * span_y) & axis_low(
                shape, 1, span_z, at_lay * span_z, n_lay * span_z
            )
            for m in range(2):
                sums = [plane_modes(ring[0, 3 + m, i])[0] for i in planes]
                for e in range(span_x + 1):
                    low = at_len * span_x + e - 1
                    there = valid & (low >= 0) & (low <= n_len * span_x - 2)
                    elem[m, e] = jnp.where(there, (sums[e] + sums[e + 1]) * 0.125, 0.0)
        below = [plane_modes(ring[s, c, planes[0]]) for c in range(3)]
        carried = None
        for e in range(span_x + 1):
            above = [plane_modes(ring[s, c, planes[e + 1]]) for c in range(3)]
            lame, shear = elem[0, e], elem[1, e]
            grad = [
                [
                    0.25 * (above[c][0] - below[c][0]),
                    0.25 * (above[c][1] + below[c][1]),
                    0.25 * (above[c][2] + below[c][2]),
                ]
                for c in range(3)
            ]
            pressure = lame * (grad[0][0] + grad[1][1] + grad[2][2])
            sheared = -0.25 * shear
            damped = (-0.125 * hourglass) * shear
            lower, upper = [], []
            for c in range(3):
                lin = [sheared * (grad[c][j] + grad[j][c]) for j in range(3)]
                lin[c] = lin[c] - 0.25 * pressure
                h_xy = damped * (above[c][1] - below[c][1])
                h_xz = damped * (above[c][2] - below[c][2])
                h_yz = damped * (above[c][3] + below[c][3])
                h_xyz = damped * (above[c][3] - below[c][3])
                lower.append([-lin[0], lin[1] - h_xy, lin[2] - h_xz, h_yz - h_xyz])
                upper.append([lin[0], lin[1] + h_xy, lin[2] + h_xz, h_yz + h_xyz])
            if e > 0:
                for c in range(3):
                    none, y, z, yz = [a + b for a, b in zip(carried[c], lower[c])]
                    even = pltpu.roll(none + z, 1, 1) + (none - z)
                    odd = pltpu.roll(y + yz, 1, 1) + (y - yz)
                    node = pltpu.roll(even + odd, 1, 0) + (even - odd)
                    inner_ref[c, e - 1] += node[0:span_y, 0:span_z]
            carried, below = upper, above

        def wait_back(o, _):
            g = (me + o) % groups
            back_copy(s, g, g).wait_recv()
            return 0

        lax.fori_loop(1, groups, wait_back, 0)
        for c in range(3):
            rows_ref[c] = lax.dot_general(
                slot_ref[...],
                back[:, c].reshape(slots, n),
                (((0,), (0,)), ((), ())),
                precision=lax.Precision.HIGHEST,
                preferred_element_type=f32,
            )
        halved_ref[...] = jnp.zeros_like(halved_ref)

        def scatter_rows(t, _):
            at = pl.ds(pl.multiple_of(t * CHUNK, CHUNK), CHUNK)
            halved_ref[...] += spread(
                [rows_ref[c, at, :] for c in range(3)], *hots(slaves_ref[at, :], span_z, tall)
            )
            return 0

        lax.fori_loop(0, pairs // CHUNK, scatter_rows, 0)
        total = joined(halved_ref[...], 3, tall)
        for i in range(span_x):
            rate = time_step / mass_ref[i]
            for c in range(3):
                force = inner_ref[c, i] + total[c][i * span_y : (i + 1) * span_y]
                speed = now_v[c, i] + rate * force
                vo_ref[c, i] = speed
                uo_ref[c, i] = now_u[c, i] + time_step * speed

    for s in range(STEPS):
        halo_sent(s)

        def sent(o, _):
            g = (me + o) % groups
            go_copy(s, g, me).wait_send()
            back_copy(s, g, me).wait_send()
            return 0

        lax.fori_loop(1, groups, sent, 0)


def per_device(
    displacement,
    velocity,
    lame_first,
    shear_modulus,
    nodal_mass,
    slave_nodes,
    initial_gap,
    candidate,
    pair_owner,
    pair_patch,
    master_faces,
):
    span_x, span_y, span_z = displacement.shape[1:]
    sizes = tuple(lax.axis_size(a) for a in ("len", "wid", "lay"))
    groups = sizes[0] * sizes[1]
    pairs, n = slave_nodes.shape[3:]
    patches = master_faces.shape[3]
    capacity = max(2, 2 * pairs // groups)
    slots = groups * capacity
    tall = span_x * span_y
    ring_y, ring_z = span_y + 8, span_z + 128
    args = (
        displacement,
        velocity,
        lame_first,
        shear_modulus,
        nodal_mass,
        slave_nodes.reshape(pairs, n),
        initial_gap.reshape(pairs, n),
        candidate.reshape(pairs, n),
        pair_owner.reshape(pairs, 1),
        pair_owner.reshape(1, pairs),
        pair_patch.reshape(pairs, 1),
        master_faces.reshape(patches, n),
    )
    block = (3, span_x, span_y, span_z)
    vm = lambda *shape: pltpu.VMEM(shape, f32)
    wide, slim = (groups, 5, capacity, n), (groups, 3, capacity, n)
    dma = lambda *shape: pltpu.SemaphoreType.DMA(shape)
    return pl.pallas_call(
        functools.partial(fused_kernel, sizes),
        out_shape=[jax.ShapeDtypeStruct(block, f32)] * 2,
        in_specs=[pl.BlockSpec(memory_space=pltpu.VMEM)] * len(args),
        out_specs=[pl.BlockSpec(memory_space=pltpu.VMEM)] * 2,
        scratch_shapes=[
            vm(STEPS, 5, span_x + 2, ring_y, ring_z),
            vm(STEPS, 2, 5, span_x, span_y, span_z),
            vm(STEPS, 2, 5, span_x, ring_z),
            vm(STEPS, 2, 5, span_x, ring_z),
            vm(2, span_x + 1, ring_y, ring_z),
            vm(slots, pairs),
            vm(3, pairs, n),
            pltpu.VMEM((slots // CHUNK, CHUNK, n), jnp.int32),
            vm(6 * tall, span_z),
            vm(*block),
            vm(*wide), vm(*slim), vm(*wide), vm(*slim),
            vm(*slim), vm(*slim), vm(*slim), vm(*slim),
            dma(STEPS, groups), dma(STEPS, groups), dma(STEPS, groups), dma(STEPS, groups),
            dma(STEPS, 3, 2), dma(STEPS, 3, 2),
        ],
        compiler_params=pltpu.CompilerParams(
            collective_id=0, has_side_effects=True, vmem_limit_bytes=48 * 1024 * 1024
        ),
    )(*args)


def solution(mesh):
    in_specs = (
        P(None, "len", "wid", "lay"),
        P(None, "len", "wid", "lay"),
        P("len", "wid", "lay"),
        P("len", "wid", "lay"),
        P("len", "wid", "lay"),
        P("len", "wid", "lay", None, None),
        P("len", "wid", "lay", None, None),
        P("len", "wid", "lay", None, None),
        P("len", "wid", "lay", None, None),
        P("len", "wid", "lay", None),
        P("len", "wid", "lay", None, None),
    )
    out_specs = (P(None, "len", "wid", "lay"), P(None, "len", "wid", "lay"))
    return jax.shard_map(
        per_device, mesh=mesh, in_specs=in_specs, out_specs=out_specs, check_vma=False
    )
```

time: 1310 us -> 64.4 us (0.05)
  local copies, waits for them, and re-layouts: 805 us -> 8.04 us
  other arithmetic: 397 us -> 0 us
  starting transfers between devices: 84.9 us -> 0 us
  Pallas kernels: 0 us -> 55 us
    gather x29 -> x0, local copies, waits for them, and re-layouts: 767 us -> none  [the longest x5 572 us: per_device(): jnp.take_along_axis(mine, jnp.broadcast_to(chosen[:, None, :], (pairs, 6,...]
    scatter-add x12 -> x0, other arithmetic: 370 us -> none  [the longest x2 93.2 us: face_sums(): summed = jnp.zeros((3, row_count * face_count), jnp.float32).at[:, flat_i...]
    pallas_call x0 -> x1, Pallas kernels: none -> 55 us  [per_device(): pl.pallas_call(functools.partial(fused_kernel, sizes), out_shape=[jax.Sha...]
    ppermute x18 -> x0, starting transfers between devices: 46 us -> none  [the longest x9 34.3 us: padded_2(): lax.ppermute(tail, axis, [(i, (i + 1) % count) for i in range(ends)])]
    all_to_all x5 -> x0, starting transfers between devices: 38.9 us -> none  [the longest x2 15.5 us: route_out(): lax.all_to_all(buffer, ('len', 'wid'), split_axis=0, concat_axis=0, tiled...]
  transfers between devices with their start and end apart: 23 -> 0, of which waited for: 6 -> 0; matrix products, arithmetic and copies ran while one was open for 19% -> 0% of each run, Pallas kernels for 0% -> 0%
where the time goes in v2:
time: 64.4 us; the launch traced here: 63.7 us
  Pallas kernels  55 us (85%)
  local copies, waits for them, and re-layouts  8.04 us (12%)
  between operations  0.68 us (1%)
    pallas_call x1, Pallas kernels, per_device(): pl.pallas_call(functools.partial(fused_kernel, sizes), out_shape=[jax.Sha...  55 us
    unnamed x22, local copies, waits for them, and re-layouts  6.47 us

profile of v2, /device:TPU:0, one launch (start us, length us, event | category | flops | bytes accessed | tf_op | source)
XLA Modules:
  0.0 63.7 jit_solution(3179963858045014243)
XLA Ops:
  0.6 0.0 copy-start
  0.6 0.8 %copy.14.patch_ref = s32[64,1]{1,0:T(8,128)S(1)} copy(s32[64,1]{0,1:T(1,128)} %bitcast.13) | data formatting | bytes 512 | tf_op jit(solution)/shard_map/reshape | solution.py:541
  1.4 0.0 copy-start.5
  1.4 0.0 copy-start.9
  1.4 0.8 %copy.13.col_ref = s32[64,1]{1,0:T(8,128)S(1)} copy(s32[64,1]{0,1:T(1,128)} %bitcast.11) | data formatting | bytes 512 | tf_op jit(solution)/shard_map/reshape | solution.py:539
  2.2 0.0 copy-done
  2.2 0.0 copy-done.5
  2.2 0.0 copy-done.9
  2.2 0.0 copy-start.1
  2.2 0.8 %copy-done.1 = f32[3,4,8,128]{3,2,1,0:T(8,128)S(1)} copy-done((f32[3,4,8,128]{3,2,1,0:T(8,128)S(1)}, f32[3,4,8,128]{3,2,1,0:T(8,128)}, u32[]{:S(2)}) %copy-start.1) | copy-done | bytes 49176
  3.0 0.0 copy-start.2
  3.0 0.8 %copy-done.2 = s32[1,1,1,64,128]{4,3,2,1,0:T(8,128)S(1)} copy-done((s32[1,1,1,64,128]{4,3,2,1,0:T(8,128)S(1)}, s32[1,1,1,64,128]{4,3,2,1,0:T(8,128)}, u32[]{:S(2)}) %copy-start.2) | copy-done | bytes 32792
  3.8 0.0 copy-start.3
  3.8 0.8 %copy-done.3 = f32[1,1,1,64,128]{4,3,2,1,0:T(8,128)S(1)} copy-done((f32[1,1,1,64,128]{4,3,2,1,0:T(8,128)S(1)}, f32[1,1,1,64,128]{4,3,2,1,0:T(8,128)}, u32[]{:S(2)}) %copy-start.3) | copy-done | bytes 32792
  4.6 0.0 copy-start.4
  4.6 0.8 %copy-done.4 = s32[1,1,1,64,128]{4,3,2,1,0:T(8,128)S(1)} copy-done((s32[1,1,1,64,128]{4,3,2,1,0:T(8,128)S(1)}, s32[1,1,1,64,128]{4,3,2,1,0:T(8,128)}, u32[]{:S(2)}) %copy-start.4) | copy-done | bytes 32792
  5.3 0.0 copy-start.6
  5.3 0.7 %copy-done.6 = f32[4,8,128]{2,1,0:T(8,128)S(1)} copy-done((f32[4,8,128]{2,1,0:T(8,128)S(1)}, f32[4,8,128]{2,1,0:T(8,128)}, u32[]{:S(2)}) %copy-start.6) | copy-done | bytes 16408
  6.0 0.0 copy-start.7
  6.0 0.7 %copy-done.7 = f32[4,8,128]{2,1,0:T(8,128)S(1)} copy-done((f32[4,8,128]{2,1,0:T(8,128)S(1)}, f32[4,8,128]{2,1,0:T(8,128)}, u32[]{:S(2)}) %copy-start.7) | copy-done | bytes 16408
  6.8 0.0 copy-start.8
  6.8 0.7 %copy-done.8 = s32[1,1,1,32,128]{4,3,2,1,0:T(8,128)S(1)} copy-done((s32[1,1,1,32,128]{4,3,2,1,0:T(8,128)S(1)}, s32[1,1,1,32,128]{4,3,2,1,0:T(8,128)}, u32[]{:S(2)}) %copy-start.8) | copy-done | bytes 16408
  7.5 55.0 %shard_map.122 = (f32[3,4,8,128]{3,2,1,0:T(8,128)S(1)}, f32[3,4,8,128]{3,2,1,0:T(8,128)S(1)}) custom-call(f32[3,4,8,128]{3,2,1,0:T(8,128)S(1)} %copy-done, f32[3,4,8,128]{3,2,1,0:T(8,128)S(1)} %copy-done.1, f32[4,8,128]{2,1,0:T(8,128)S(1)} %copy-done.5, f32[4,8,128]{2,1,0:T(8,128)S(1)} %copy-done.6, f32[4,8,128]{2,1,0:T(8,128)S(1)} %copy-done.7, ...), custom_call_target="tpu_custom_call" | custom-call | tf_op jit(solution)/shard_map/pallas_call | solution.py:548
  62.5 0.6 copy.17
  63.1 0.6 copy.18
Async XLA Ops:
  0.6 1.6 %copy-start = (f32[3,4,8,128]{3,2,1,0:T(8,128)S(1)}, f32[3,4,8,128]{3,2,1,0:T(8,128)}, u32[]{:S(2)}) copy-start(f32[3,4,8,128]{3,2,1,0:T(8,128)} %u_ref.1) | copy-start | bytes 147460
  1.4 0.8 %copy-start.5 = (f32[4,8,128]{2,1,0:T(8,128)S(1)}, f32[4,8,128]{2,1,0:T(8,128)}, u32[]{:S(2)}) copy-start(f32[4,8,128]{2,1,0:T(8,128)} %lame_ref.1) | copy-start | bytes 49156
  1.4 0.8 %copy-start.9 = (s32[1,1,1,64,1]{3,4,2,1,0:T(1,128)S(1)}, s32[1,1,1,64,1]{3,4,2,1,0:T(1,128)}, u32[]{:S(2)}) copy-start(s32[1,1,1,64,1]{3,4,2,1,0:T(1,128)} %param.19) | copy-start | bytes 772
  2.2 0.8 %copy-start.1 = (f32[3,4,8,128]{3,2,1,0:T(8,128)S(1)}, f32[3,4,8,128]{3,2,1,0:T(8,128)}, u32[]{:S(2)}) copy-start(f32[3,4,8,128]{3,2,1,0:T(8,128)} %v_ref.1) | copy-start | bytes 147460
  3.0 0.8 %copy-start.2 = (s32[1,1,1,64,128]{4,3,2,1,0:T(8,128)S(1)}, s32[1,1,1,64,128]{4,3,2,1,0:T(8,128)}, u32[]{:S(2)}) copy-start(s32[1,1,1,64,128]{4,3,2,1,0:T(8,128)} %param.16) | copy-start | bytes 98308
  3.8 0.8 %copy-start.3 = (f32[1,1,1,64,128]{4,3,2,1,0:T(8,128)S(1)}, f32[1,1,1,64,128]{4,3,2,1,0:T(8,128)}, u32[]{:S(2)}) copy-start(f32[1,1,1,64,128]{4,3,2,1,0:T(8,128)} %param.17) | copy-start | bytes 98308
  4.6 0.8 %copy-start.4 = (s32[1,1,1,64,128]{4,3,2,1,0:T(8,128)S(1)}, s32[1,1,1,64,128]{4,3,2,1,0:T(8,128)}, u32[]{:S(2)}) copy-start(s32[1,1,1,64,128]{4,3,2,1,0:T(8,128)} %param.18) | copy-start | bytes 98308
  5.3 0.7 %copy-start.6 = (f32[4,8,128]{2,1,0:T(8,128)S(1)}, f32[4,8,128]{2,1,0:T(8,128)}, u32[]{:S(2)}) copy-start(f32[4,8,128]{2,1,0:T(8,128)} %shear_ref.1) | copy-start | bytes 49156
  6.0 0.7 %copy-start.7 = (f32[4,8,128]{2,1,0:T(8,128)S(1)}, f32[4,8,128]{2,1,0:T(8,128)}, u32[]{:S(2)}) copy-start(f32[4,8,128]{2,1,0:T(8,128)} %mass_ref.1) | copy-start | bytes 49156
  6.8 0.7 %copy-start.8 = (s32[1,1,1,32,128]{4,3,2,1,0:T(8,128)S(1)}, s32[1,1,1,32,128]{4,3,2,1,0:T(8,128)}, u32[]{:S(2)}) copy-start(s32[1,1,1,32,128]{4,3,2,1,0:T(8,128)} %param.21) | copy-start | bytes 49156

commit v3 on v2

--- a/solution.py
+++ b/solution.py
@@ -167,12 +167,14 @@
 
 def fused_kernel(
     sizes,
-    u_ref, v_ref, lame_ref, shear_ref, mass_ref, slaves_ref, gap_ref, chosen_ref, col_ref, row_ref,
-    patch_ref, faces_ref,
+    u_hbm, v_hbm, lame_hbm, shear_hbm, mass_hbm, slaves_hbm, gap_hbm, chosen_hbm, row_hbm,
+    patch_hbm, faces_hbm,
     uo_ref, vo_ref,
+    u_ref, v_ref, lame_ref, shear_ref, mass_ref, slaves_ref, gap_ref, chosen_ref, row_ref,
+    patch_ref, faces_ref, load_sem,
     ring, z_in, y_out, y_in, elem, slot_ref, rows_ref, nodes_ref, halved_ref, inner_ref,
-    out_1, out_2, in_1, in_2, force_1, force_2, back_1, back_2,
-    go_send, go_recv, back_send, back_recv, halo_send, halo_recv,
+    fix_out, fix_in, out_1, out_2, in_1, in_2, force_1, force_2, back_1, back_2,
+    fix_send, fix_recv, go_send, go_recv, back_send, back_recv, halo_send, halo_recv,
 ):
     n_len, n_wid, n_lay = sizes
     groups = n_len * n_wid
@@ -184,11 +186,27 @@
     pairs = slaves_ref.shape[0]
     patches = faces_ref.shape[0]
     ring_y, ring_z = ring.shape[3:]
+    blocks = groups // per
+    side_by = 2 if blocks % 2 == 0 and pairs // CHUNK % 2 == 0 else 1
     at_len, at_wid, at_lay = lax.axis_index("len"), lax.axis_index("wid"), lax.axis_index("lay")
     me = at_len * n_wid + at_wid
 
     def peer_id(g):
         return (g // n_wid, g % n_wid, at_lay)
+
+    loads = [
+        pltpu.make_async_copy(src, dst, load_sem.at[i])
+        for i, (src, dst) in enumerate(
+            (
+                (row_hbm, row_ref), (patch_hbm, patch_ref), (gap_hbm, gap_ref),
+                (chosen_hbm, chosen_ref), (u_hbm, u_ref), (slaves_hbm, slaves_ref),
+                (lame_hbm, lame_ref), (shear_hbm, shear_ref), (faces_hbm, faces_ref),
+                (v_hbm, v_ref), (mass_hbm, mass_ref),
+            )
+        )
+    ]
+    for load in loads:
+        load.start()
 
     zero_plane = jnp.zeros((ring_y, ring_z), f32)
     for s in range(STEPS):
@@ -209,6 +227,8 @@
     for other in lay_peers:
         pl.semaphore_signal(barrier, inc=1, device_id=(at_len, at_wid, other), device_id_type=MESH)
     pl.semaphore_wait(barrier, groups - 1 + len(lay_peers))
+    for load in loads:
+        load.wait()
 
     def halo_copy(s, phase, side):
         comps = pl.ds(0, 5 if s == 0 else 3)
@@ -264,6 +284,16 @@
                 def _():
                     copy.wait_send()
 
+    def fix_copy(g, slot):
+        return pltpu.make_async_remote_copy(
+            src_ref=fix_out.at[g],
+            dst_ref=fix_in.at[slot],
+            send_sem=fix_send.at[g],
+            recv_sem=fix_recv.at[slot],
+            device_id=peer_id(g),
+            device_id_type=MESH,
+        )
+
     def go_copy(s, g, slot):
         return pltpu.make_async_remote_copy(
             src_ref=(out_1, out_2)[s].at[g],
@@ -298,6 +328,23 @@
     lanes_z = lax.broadcasted_iota(jnp.int32, (span_y, span_z), 1)
     rows_y = lax.broadcasted_iota(jnp.int32, (ring_y - span_y, ring_z), 0)
 
+    diagonal = lax.broadcasted_iota(jnp.int32, (pairs, pairs), 0) == lax.broadcasted_iota(
+        jnp.int32, (pairs, pairs), 1
+    )
+
+    def column(row):
+        return jnp.sum(jnp.where(diagonal, row.astype(f32), 0.0), axis=1, keepdims=True).astype(
+            jnp.int32
+        )
+
+    row = row_ref[...]
+    to_slot = slot_matrix(column(row), row, capacity, slots)
+    slot_ref[...] = jnp.concatenate([to_slot, to_slot], axis=1).astype(bf16)
+    face_id = (column(patch_ref[...]) * n + chosen_ref[...] + 1).astype(f32)
+    fix_out[:, 0] = to_groups(exact_dot(to_slot, gap_ref[...]))
+    fix_out[:, 1] = to_groups(exact_dot(to_slot, face_id) - 1.0)
+    fix_in[me] = fix_out[me]
+
     for s in range(STEPS):
         comps = 5 if s == 0 else 3
         now_u, now_v = (u_ref, v_ref) if s == 0 else (uo_ref, vo_ref)
@@ -310,25 +357,36 @@
                     now_u[c, i] if c < 3 else (lame_ref, shear_ref)[c - 3][i]
                 )
         halo_start(s, 0)
+        if s == 0:
+
+            def send_fix(o, _):
+                fix_copy((me + o) % groups, me).start()
+                return 0
+
+            lax.fori_loop(1, groups, send_fix, 0)
 
         u = now_u[...]
         table = as_table([flat_block(u, c) for c in range(3)])
 
+        to_slots = slot_ref[...]
+
         def gather_rows(t, _):
-            at = pl.ds(pl.multiple_of(t * CHUNK, CHUNK), CHUNK)
-            got = pick(table, *hots(slaves_ref[at, :], span_z, tall), 3)
-            for c in range(3):
-                rows_ref[c, at, :] = got[c]
+            for q in range(side_by):
+                at = pl.ds(pl.multiple_of((t * side_by + q) * CHUNK, CHUNK), CHUNK)
+                got = pick(table, *hots(slaves_ref[at, :], span_z, tall), 3)
+                for c in range(3):
+                    rows_ref[c, at, :] = got[c]
             return 0
 
-        lax.fori_loop(0, pairs // CHUNK, gather_rows, 0)
-        if s == 0:
-            slot_ref[...] = slot_matrix(col_ref[...], row_ref[...], capacity, slots)
-            face_id = (patch_ref[...] * n + chosen_ref[...] + 1).astype(f32)
-            out[:, 3] = to_groups(exact_dot(slot_ref[...], gap_ref[...]))
-            out[:, 4] = to_groups(exact_dot(slot_ref[...], face_id) - 1.0)
+        lax.fori_loop(0, pairs // CHUNK // side_by, gather_rows, 0)
+        both = [halves(rows_ref[c]) for c in range(3)]
+        moved = jnp.dot(
+            to_slots,
+            jnp.concatenate([jnp.concatenate([b[k] for b in both], axis=1) for k in range(2)], axis=0),
+            preferred_element_type=f32,
+        )
         for c in range(3):
-            out[:, c] = to_groups(exact_dot(slot_ref[...], rows_ref[c]))
+            out[:, c] = to_groups(moved[:, c * n : (c + 1) * n])
         into[me] = out[me]
 
         def send_go(o, _):
@@ -367,41 +425,119 @@
                 ring[s, c, i, span_y:ring_y, :] = tile
         halo_start(s, 2)
 
+        planes = [span_x + 1] + list(range(span_x + 1))
+        shape = (ring_y, ring_z)
+
+        def material(e):
+            valid = axis_low(shape, 0, span_y, at_wid * span_y, n_wid * span_y) & axis_low(
+                shape, 1, span_z, at_lay * span_z, n_lay * span_z
+            )
+            low = at_len * span_x + e - 1
+            there = valid & (low >= 0) & (low <= n_len * span_x - 2)
+            for m in range(2):
+                sums = [plane_modes(ring[0, 3 + m, planes[e + k]])[0] for k in range(2)]
+                elem[m, e] = jnp.where(there, (sums[0] + sums[1]) * 0.125, 0.0)
+
+        def settle(i, modes):
+            for c in range(3):
+                none, y, z, yz = modes[c]
+                even = pltpu.roll(none + z, 1, 1) + (none - z)
+                odd = pltpu.roll(y + yz, 1, 1) + (y - yz)
+                node = pltpu.roll(even + odd, 1, 0) + (even - odd)
+                inner_ref[c, i] += node[0:span_y, 0:span_z]
+
+        def internal(elements):
+            carried, last = None, None
+            for e in elements:
+                if s == 0:
+                    material(e)
+                if e - 1 == last:
+                    below = above
+                else:
+                    if carried is not None and last < span_x:
+                        settle(last, carried)
+                    carried = None
+                    below = [plane_modes(ring[s, c, planes[e]]) for c in range(3)]
+                above = [plane_modes(ring[s, c, planes[e + 1]]) for c in range(3)]
+                lame, shear = elem[0, e], elem[1, e]
+                grad = [
+                    [
+                        0.25 * (above[c][0] - below[c][0]),
+                        0.25 * (above[c][1] + below[c][1]),
+                        0.25 * (above[c][2] + below[c][2]),
+                    ]
+                    for c in range(3)
+                ]
+                pressure = lame * (grad[0][0] + grad[1][1] + grad[2][2])
+                sheared = -0.25 * shear
+                damped = (-0.125 * hourglass) * shear
+                lower, upper = [], []
+                for c in range(3):
+                    lin = [sheared * (grad[c][j] + grad[j][c]) for j in range(3)]
+                    lin[c] = lin[c] - 0.25 * pressure
+                    h_xy = damped * (above[c][1] - below[c][1])
+                    h_xz = damped * (above[c][2] - below[c][2])
+                    h_yz = damped * (above[c][3] + below[c][3])
+                    h_xyz = damped * (above[c][3] - below[c][3])
+                    lower.append([-lin[0], lin[1] - h_xy, lin[2] - h_xz, h_yz - h_xyz])
+                    upper.append([lin[0], lin[1] + h_xy, lin[2] + h_xz, h_yz + h_xyz])
+                if e > 0:
+                    if carried is None:
+                        settle(e - 1, lower)
+                    else:
+                        settle(e - 1, [[p + q for p, q in zip(carried[c], lower[c])] for c in range(3)])
+                carried, last = upper, e
+            if last < span_x:
+                settle(last, carried)
+
+        inner_ref[...] = jnp.zeros_like(inner_ref)
+        internal(list(range(1, span_x)))
+
+        def landed(t):
+            return [(me // per - t * side_by - q + 2 * blocks) % blocks for q in range(side_by)]
+
+        def others(t, act):
+            for b in landed(t):
+                for k in range(per):
+                    g = b * per + k
+
+                    @pl.when(g != me)
+                    def _():
+                        act(g)
+
+        if s == 0:
+
+            def resolve(t, _):
+                others(t, lambda g: fix_copy(g, g).wait_recv())
+                for b in landed(t):
+                    face_id = held(fix_in, b, 1).astype(jnp.int32)
+                    high, low = pick(face_table, *hots(face_id, n, patches), 2)
+                    node = high.astype(jnp.int32) * span_z + low.astype(jnp.int32)
+                    nodes_ref[b] = jnp.where(face_id < 0, -1, node)
+                return 0
+
+            lax.fori_loop(0, blocks // side_by, resolve, 0)
+
         def own(t, _):
-            b = (me // per - t + groups // per) % (groups // per)
-            for k in range(per):
-                g = b * per + k
-
-                @pl.when(g != me)
-                def _():
-                    go_copy(s, g, g).wait_recv()
-
-            if s == 0:
-                face_id = held(in_1, b, 4).astype(jnp.int32)
-                high, low = pick(face_table, *hots(face_id, n, patches), 2)
-                node = high.astype(jnp.int32) * span_z + low.astype(jnp.int32)
-                nodes_ref[b] = jnp.where(face_id < 0, -1, node)
-            lane_hot, match = hots(nodes_ref[b], span_z, tall)
-            got = pick(frame_table, lane_hot, match, 6)
-            gap = held(in_1, b, 3)
-            for c in range(3):
-                gap = gap + (held(into, b, c) - got[c]) * got[3 + c]
-            push = -penalty * jnp.minimum(gap, 0.0)
-            force = [push * got[3 + c] for c in range(3)]
-            for c in range(3):
-                for k in range(per):
-                    force_ref[b * per + k, c] = force[c][k * capacity : (k + 1) * capacity]
-            for k in range(per):
-                g = b * per + k
-
-                @pl.when(g != me)
-                def _():
-                    back_copy(s, g, me).start()
-
-            halved_ref[...] += spread(force, lane_hot, match)
+            others(t, lambda g: go_copy(s, g, g).wait_recv())
+            added = []
+            for b in landed(t):
+                lane_hot, match = hots(nodes_ref[b], span_z, tall)
+                got = pick(frame_table, lane_hot, match, 6)
+                gap = held(fix_in, b, 0)
+                for c in range(3):
+                    gap = gap + (held(into, b, c) - got[c]) * got[3 + c]
+                push = -penalty * jnp.minimum(gap, 0.0)
+                force = [push * got[3 + c] for c in range(3)]
+                for c in range(3):
+                    for k in range(per):
+                        force_ref[b * per + k, c] = force[c][k * capacity : (k + 1) * capacity]
+                added.append(spread(force, lane_hot, match))
+            others(t, lambda g: back_copy(s, g, me).start())
+            halved_ref[...] += functools.reduce(jnp.add, added)
             return 0
 
-        lax.fori_loop(0, groups // per, own, 0)
+        lax.fori_loop(0, blocks // side_by, own, 0)
         back[me] = force_ref[me]
 
         total = joined(halved_ref[...], 3, tall)
@@ -410,55 +546,10 @@
             quarter = [-0.25 * total[c][i * span_y : (i + 1) * span_y] for i in range(span_x)]
             for i in range(span_x):
                 both = (quarter[i] if i < span_x - 1 else zero) + (quarter[i - 1] if i else zero)
-                inner_ref[c, i] = both + pltpu.roll(both, 1, 0)
+                inner_ref[c, i] += both + pltpu.roll(both, 1, 0)
 
         halo_wait(s, 2)
-        planes = [span_x + 1] + list(range(span_x + 1))
-        if s == 0:
-            shape = (ring_y, ring_z)
-            valid = axis_low(shape, 0, span_y, at_wid * span_y, n_wid * span_y) & axis_low(
-                shape, 1, span_z, at_lay * span_z, n_lay * span_z
-            )
-            for m in range(2):
-                sums = [plane_modes(ring[0, 3 + m, i])[0] for i in planes]
-                for e in range(span_x + 1):
-                    low = at_len * span_x + e - 1
-                    there = valid & (low >= 0) & (low <= n_len * span_x - 2)
-                    elem[m, e] = jnp.where(there, (sums[e] + sums[e + 1]) * 0.125, 0.0)
-        below = [plane_modes(ring[s, c, planes[0]]) for c in range(3)]
-        carried = None
-        for e in range(span_x + 1):
-            above = [plane_modes(ring[s, c, planes[e + 1]]) for c in range(3)]
-            lame, shear = elem[0, e], elem[1, e]
-            grad = [
-                [
-                    0.25 * (above[c][0] - below[c][0]),
-                    0.25 * (above[c][1] + below[c][1]),
-                    0.25 * (above[c][2] + below[c][2]),
-                ]
-                for c in range(3)
-            ]
-            pressure = lame * (grad[0][0] + grad[1][1] + grad[2][2])
-            sheared = -0.25 * shear
-            damped = (-0.125 * hourglass) * shear
-            lower, upper = [], []
-            for c in range(3):
-                lin = [sheared * (grad[c][j] + grad[j][c]) for j in range(3)]
-                lin[c] = lin[c] - 0.25 * pressure
-                h_xy = damped * (above[c][1] - below[c][1])
-                h_xz = damped * (above[c][2] - below[c][2])
-                h_yz = damped * (above[c][3] + below[c][3])
-                h_xyz = damped * (above[c][3] - below[c][3])
-                lower.append([-lin[0], lin[1] - h_xy, lin[2] - h_xz, h_yz - h_xyz])
-                upper.append([lin[0], lin[1] + h_xy, lin[2] + h_xz, h_yz + h_xyz])
-            if e > 0:
-                for c in range(3):
-                    none, y, z, yz = [a + b for a, b in zip(carried[c], lower[c])]
-                    even = pltpu.roll(none + z, 1, 1) + (none - z)
-                    odd = pltpu.roll(y + yz, 1, 1) + (y - yz)
-                    node = pltpu.roll(even + odd, 1, 0) + (even - odd)
-                    inner_ref[c, e - 1] += node[0:span_y, 0:span_z]
-            carried, below = upper, above
+        internal([0, span_x])
 
         def wait_back(o, _):
             g = (me + o) % groups
@@ -466,24 +557,31 @@
             return 0
 
         lax.fori_loop(1, groups, wait_back, 0)
+        both = [halves(back[:, c].reshape(slots, n)) for c in range(3)]
+        moved = lax.dot_general(
+            to_slots[:, 0:pairs],
+            jnp.concatenate([b[k] for k in range(2) for b in both], axis=1),
+            (((0,), (0,)), ((), ())),
+            preferred_element_type=f32,
+        )
         for c in range(3):
-            rows_ref[c] = lax.dot_general(
-                slot_ref[...],
-                back[:, c].reshape(slots, n),
-                (((0,), (0,)), ((), ())),
-                precision=lax.Precision.HIGHEST,
-                preferred_element_type=f32,
-            )
+            rows_ref[c] = moved[:, c * n : (c + 1) * n] + moved[:, (3 + c) * n : (4 + c) * n]
         halved_ref[...] = jnp.zeros_like(halved_ref)
 
         def scatter_rows(t, _):
-            at = pl.ds(pl.multiple_of(t * CHUNK, CHUNK), CHUNK)
-            halved_ref[...] += spread(
-                [rows_ref[c, at, :] for c in range(3)], *hots(slaves_ref[at, :], span_z, tall)
-            )
+            added = []
+            for q in range(side_by):
+                at = pl.ds(pl.multiple_of((t * side_by + q) * CHUNK, CHUNK), CHUNK)
+                added.append(
+                    spread(
+                        [rows_ref[c, at, :] for c in range(3)],
+                        *hots(slaves_ref[at, :], span_z, tall),
+                    )
+                )
+            halved_ref[...] += functools.reduce(jnp.add, added)
             return 0
 
-        lax.fori_loop(0, pairs // CHUNK, scatter_rows, 0)
+        lax.fori_loop(0, pairs // CHUNK // side_by, scatter_rows, 0)
         total = joined(halved_ref[...], 3, tall)
         for i in range(span_x):
             rate = time_step / mass_ref[i]
@@ -498,6 +596,8 @@
 
         def sent(o, _):
             g = (me + o) % groups
+            if s == 0:
+                fix_copy(g, me).wait_send()
             go_copy(s, g, me).wait_send()
             back_copy(s, g, me).wait_send()
             return 0
@@ -536,33 +636,35 @@
         slave_nodes.reshape(pairs, n),
         initial_gap.reshape(pairs, n),
         candidate.reshape(pairs, n),
-        pair_owner.reshape(pairs, 1),
         pair_owner.reshape(1, pairs),
-        pair_patch.reshape(pairs, 1),
+        pair_patch.reshape(1, pairs),
         master_faces.reshape(patches, n),
     )
     block = (3, span_x, span_y, span_z)
     vm = lambda *shape: pltpu.VMEM(shape, f32)
-    wide, slim = (groups, 5, capacity, n), (groups, 3, capacity, n)
+    fixed, slim = (groups, 2, capacity, n), (groups, 3, capacity, n)
     dma = lambda *shape: pltpu.SemaphoreType.DMA(shape)
     return pl.pallas_call(
         functools.partial(fused_kernel, sizes),
         out_shape=[jax.ShapeDtypeStruct(block, f32)] * 2,
-        in_specs=[pl.BlockSpec(memory_space=pltpu.VMEM)] * len(args),
+        in_specs=[pl.BlockSpec(memory_space=pltpu.HBM)] * len(args),
         out_specs=[pl.BlockSpec(memory_space=pltpu.VMEM)] * 2,
         scratch_shapes=[
+            *[pltpu.VMEM(a.shape, a.dtype) for a in args],
+            dma(len(args)),
             vm(STEPS, 5, span_x + 2, ring_y, ring_z),
             vm(STEPS, 2, 5, span_x, span_y, span_z),
             vm(STEPS, 2, 5, span_x, ring_z),
             vm(STEPS, 2, 5, span_x, ring_z),
             vm(2, span_x + 1, ring_y, ring_z),
-            vm(slots, pairs),
+            pltpu.VMEM((slots, 2 * pairs), bf16),
             vm(3, pairs, n),
             pltpu.VMEM((slots // CHUNK, CHUNK, n), jnp.int32),
             vm(6 * tall, span_z),
             vm(*block),
-            vm(*wide), vm(*slim), vm(*wide), vm(*slim),
+            vm(*fixed), vm(*fixed), vm(*slim), vm(*slim), vm(*slim), vm(*slim),
             vm(*slim), vm(*slim), vm(*slim), vm(*slim),
+            dma(groups), dma(groups),
             dma(STEPS, groups), dma(STEPS, groups), dma(STEPS, groups), dma(STEPS, groups),
             dma(STEPS, 3, 2), dma(STEPS, 3, 2),
         ],

time: 64.4 us -> 57.5 us (0.89)
  Pallas kernels: 55 us -> 47.6 us
    pallas_call x1, Pallas kernels: 55 us -> 47.6 us  [per_device(): pl.pallas_call(functools.partial(fused_kernel, sizes), out_shape=[jax.Sha...]
    unnamed x22 -> x24, local copies, waits for them, and re-layouts: 6.47 us -> 8.63 us
    reshape x2 -> x0, local copies, waits for them, and re-layouts: 1.57 us -> none  [the longest x1 0.81 us: per_device(): pair_owner.reshape(pairs, 1)]
where the time goes in v3:
time: 57.5 us; the launch traced here: 56.9 us
  Pallas kernels  47.6 us (83%)
  local copies, waits for them, and re-layouts  8.63 us (15%)
  between operations  0.67 us (1%)
    pallas_call x1, Pallas kernels, per_device(): pl.pallas_call(functools.partial(fused_kernel, sizes), out_shape=[jax.Sha...  47.6 us
    unnamed x24, local copies, waits for them, and re-layouts  8.63 us

profile of v3, /device:TPU:0, one launch (start us, length us, event | category | flops | bytes accessed | tf_op | source)
XLA Modules:
  0.0 56.9 jit_solution(3512589060259871237)
XLA Ops:
  0.6 0.0 copy-start.9
  0.6 0.0 copy-start.10
  0.7 0.6 %copy-done.9 = s32[1,1,1,64,1]{3,4,2,1,0:T(1,128)S(1)} copy-done((s32[1,1,1,64,1]{3,4,2,1,0:T(1,128)S(1)}, s32[1,1,1,64,1]{3,4,2,1,0:T(1,128)}, u32[]{:S(2)}) %copy-start.9) | copy-done | bytes 280
  1.3 0.0 copy-done.10
  1.3 0.0 copy-start
  1.3 0.8 %copy-done = f32[3,4,8,128]{3,2,1,0:T(8,128)S(1)} copy-done((f32[3,4,8,128]{3,2,1,0:T(8,128)S(1)}, f32[3,4,8,128]{3,2,1,0:T(8,128)}, u32[]{:S(2)}) %copy-start) | copy-done | bytes 49176
  2.1 0.0 copy-start.1
  2.1 0.8 %copy-done.1 = f32[3,4,8,128]{3,2,1,0:T(8,128)S(1)} copy-done((f32[3,4,8,128]{3,2,1,0:T(8,128)S(1)}, f32[3,4,8,128]{3,2,1,0:T(8,128)}, u32[]{:S(2)}) %copy-start.1) | copy-done | bytes 49176
  2.9 0.0 copy-start.2
  2.9 0.8 %copy-done.2 = s32[1,1,1,64,128]{4,3,2,1,0:T(8,128)S(1)} copy-done((s32[1,1,1,64,128]{4,3,2,1,0:T(8,128)S(1)}, s32[1,1,1,64,128]{4,3,2,1,0:T(8,128)}, u32[]{:S(2)}) %copy-start.2) | copy-done | bytes 32792
  3.7 0.0 copy-start.3
  3.7 0.8 %copy-done.3 = f32[1,1,1,64,128]{4,3,2,1,0:T(8,128)S(1)} copy-done((f32[1,1,1,64,128]{4,3,2,1,0:T(8,128)S(1)}, f32[1,1,1,64,128]{4,3,2,1,0:T(8,128)}, u32[]{:S(2)}) %copy-start.3) | copy-done | bytes 32792
  4.4 0.0 copy-start.4
  4.4 0.8 %copy-done.4 = s32[1,1,1,64,128]{4,3,2,1,0:T(8,128)S(1)} copy-done((s32[1,1,1,64,128]{4,3,2,1,0:T(8,128)S(1)}, s32[1,1,1,64,128]{4,3,2,1,0:T(8,128)}, u32[]{:S(2)}) %copy-start.4) | copy-done | bytes 32792
  5.2 0.0 copy-start.5
  5.2 0.7 %copy-done.5 = f32[4,8,128]{2,1,0:T(8,128)S(1)} copy-done((f32[4,8,128]{2,1,0:T(8,128)S(1)}, f32[4,8,128]{2,1,0:T(8,128)}, u32[]{:S(2)}) %copy-start.5) | copy-done | bytes 16408
  5.9 0.0 copy-start.6
  5.9 0.7 %copy-done.6 = f32[4,8,128]{2,1,0:T(8,128)S(1)} copy-done((f32[4,8,128]{2,1,0:T(8,128)S(1)}, f32[4,8,128]{2,1,0:T(8,128)}, u32[]{:S(2)}) %copy-start.6) | copy-done | bytes 16408
  6.6 0.0 copy-start.7
  6.6 0.7 %copy-done.7 = f32[4,8,128]{2,1,0:T(8,128)S(1)} copy-done((f32[4,8,128]{2,1,0:T(8,128)S(1)}, f32[4,8,128]{2,1,0:T(8,128)}, u32[]{:S(2)}) %copy-start.7) | copy-done | bytes 16408
  7.3 0.0 copy-start.8
  7.3 0.7 %copy-done.8 = s32[1,1,1,32,128]{4,3,2,1,0:T(8,128)S(1)} copy-done((s32[1,1,1,32,128]{4,3,2,1,0:T(8,128)S(1)}, s32[1,1,1,32,128]{4,3,2,1,0:T(8,128)}, u32[]{:S(2)}) %copy-start.8) | copy-done | bytes 16408
  8.1 47.6 %shard_map.122 = (f32[3,4,8,128]{3,2,1,0:T(8,128)S(1)}, f32[3,4,8,128]{3,2,1,0:T(8,128)S(1)}) custom-call(f32[3,4,8,128]{3,2,1,0:T(8,128)S(1)} %copy-done, f32[3,4,8,128]{3,2,1,0:T(8,128)S(1)} %copy-done.1, f32[4,8,128]{2,1,0:T(8,128)S(1)} %copy-done.5, f32[4,8,128]{2,1,0:T(8,128)S(1)} %copy-done.6, f32[4,8,128]{2,1,0:T(8,128)S(1)} %copy-done.7, ...), custom_call_target="tpu_custom_call" | custom-call | tf_op jit(solution)/shard_map/pallas_call | solution.py:647
  55.6 0.6 %copy.15 = f32[3,4,8,128]{3,2,1,0:T(8,128)} copy(f32[3,4,8,128]{3,2,1,0:T(8,128)S(1)} %get-tuple-element.4) | data formatting | bytes 98304
  56.2 0.6 %copy.16 = f32[3,4,8,128]{3,2,1,0:T(8,128)} copy(f32[3,4,8,128]{3,2,1,0:T(8,128)S(1)} %get-tuple-element.5) | data formatting | bytes 98304
Async XLA Ops:
  0.6 0.7 %copy-start.9 = (s32[1,1,1,64,1]{3,4,2,1,0:T(1,128)S(1)}, s32[1,1,1,64,1]{3,4,2,1,0:T(1,128)}, u32[]{:S(2)}) copy-start(s32[1,1,1,64,1]{3,4,2,1,0:T(1,128)} %param.19) | copy-start | bytes 772
  0.6 0.7 %copy-start.10 = (s32[1,1,1,64]{3,2,1,0:T(1,128)S(1)}, s32[1,1,1,64]{3,2,1,0:T(1,128)}, u32[]{:S(2)}) copy-start(s32[1,1,1,64]{3,2,1,0:T(1,128)} %param.20) | copy-start | bytes 772
  1.3 0.8 %copy-start = (f32[3,4,8,128]{3,2,1,0:T(8,128)S(1)}, f32[3,4,8,128]{3,2,1,0:T(8,128)}, u32[]{:S(2)}) copy-start(f32[3,4,8,128]{3,2,1,0:T(8,128)} %u_hbm.1) | copy-start | bytes 147460
  2.1 0.8 %copy-start.1 = (f32[3,4,8,128]{3,2,1,0:T(8,128)S(1)}, f32[3,4,8,128]{3,2,1,0:T(8,128)}, u32[]{:S(2)}) copy-start(f32[3,4,8,128]{3,2,1,0:T(8,128)} %v_hbm.1) | copy-start | bytes 147460
  2.9 0.8 %copy-start.2 = (s32[1,1,1,64,128]{4,3,2,1,0:T(8,128)S(1)}, s32[1,1,1,64,128]{4,3,2,1,0:T(8,128)}, u32[]{:S(2)}) copy-start(s32[1,1,1,64,128]{4,3,2,1,0:T(8,128)} %param.16) | copy-start | bytes 98308
  3.7 0.8 %copy-start.3 = (f32[1,1,1,64,128]{4,3,2,1,0:T(8,128)S(1)}, f32[1,1,1,64,128]{4,3,2,1,0:T(8,128)}, u32[]{:S(2)}) copy-start(f32[1,1,1,64,128]{4,3,2,1,0:T(8,128)} %param.17) | copy-start | bytes 98308
  4.4 0.8 %copy-start.4 = (s32[1,1,1,64,128]{4,3,2,1,0:T(8,128)S(1)}, s32[1,1,1,64,128]{4,3,2,1,0:T(8,128)}, u32[]{:S(2)}) copy-start(s32[1,1,1,64,128]{4,3,2,1,0:T(8,128)} %param.18) | copy-start | bytes 98308
  5.2 0.7 %copy-start.5 = (f32[4,8,128]{2,1,0:T(8,128)S(1)}, f32[4,8,128]{2,1,0:T(8,128)}, u32[]{:S(2)}) copy-start(f32[4,8,128]{2,1,0:T(8,128)} %lame_hbm.1) | copy-start | bytes 49156
  5.9 0.7 %copy-start.6 = (f32[4,8,128]{2,1,0:T(8,128)S(1)}, f32[4,8,128]{2,1,0:T(8,128)}, u32[]{:S(2)}) copy-start(f32[4,8,128]{2,1,0:T(8,128)} %shear_hbm.1) | copy-start | bytes 49156
  6.6 0.7 %copy-start.7 = (f32[4,8,128]{2,1,0:T(8,128)S(1)}, f32[4,8,128]{2,1,0:T(8,128)}, u32[]{:S(2)}) copy-start(f32[4,8,128]{2,1,0:T(8,128)} %mass_hbm.1) | copy-start | bytes 49156
  7.3 0.7 %copy-start.8 = (s32[1,1,1,32,128]{4,3,2,1,0:T(8,128)S(1)}, s32[1,1,1,32,128]{4,3,2,1,0:T(8,128)}, u32[]{:S(2)}) copy-start(s32[1,1,1,32,128]{4,3,2,1,0:T(8,128)} %param.21) | copy-start | bytes 49156

commit v4 on v3

--- a/solution.py
+++ b/solution.py
@@ -669,7 +669,7 @@
             dma(STEPS, 3, 2), dma(STEPS, 3, 2),
         ],
         compiler_params=pltpu.CompilerParams(
-            collective_id=0, has_side_effects=True, vmem_limit_bytes=48 * 1024 * 1024
+            collective_id=0, has_side_effects=True, vmem_limit_bytes=64 * 1024 * 1024
         ),
     )(*args)
 

time: 57.5 us -> 50.8 us (0.88)
  local copies, waits for them, and re-layouts: 8.63 us -> 2.06 us
    unnamed x24 -> x4, local copies, waits for them, and re-layouts: 8.63 us -> 2.06 us
where the time goes in v4:
time: 50.8 us; the launch traced here: 50.6 us
  Pallas kernels  47.9 us (94%)
  local copies, waits for them, and re-layouts  2.06 us (4%)
  between operations  0.65 us (1%)
    pallas_call x1, Pallas kernels, per_device(): pl.pallas_call(functools.partial(fused_kernel, sizes), out_shape=[jax.Sha...  47.9 us
    unnamed x4, local copies, waits for them, and re-layouts  2.06 us

profile of v4, /device:TPU:0, one launch (start us, length us, event | category | flops | bytes accessed | tf_op | source)
XLA Modules:
  0.0 50.6 jit_solution(4489432178397158946)
XLA Ops:
  0.6 47.9 %shard_map.122 = (f32[3,4,8,128]{3,2,1,0:T(8,128)}, f32[3,4,8,128]{3,2,1,0:T(8,128)}) custom-call(f32[3,4,8,128]{3,2,1,0:T(8,128)} %u_hbm.1, f32[3,4,8,128]{3,2,1,0:T(8,128)} %v_hbm.1, f32[4,8,128]{2,1,0:T(8,128)} %lame_hbm.1, f32[4,8,128]{2,1,0:T(8,128)} %shear_hbm.1, f32[4,8,128]{2,1,0:T(8,128)} %mass_hbm.1, s32[64,128]{1,0:T(8,128)} %bitcast.6, ...), custom_call_target="tpu_custom_call" | custom-call | tf_op jit(solution)/shard_map/pallas_call | solution.py:647
  48.5 0.0 copy-start
  48.5 1.4 %copy.15 = f32[3,4,8,128]{3,2,1,0:T(8,128)} copy(f32[3,4,8,128]{3,2,1,0:T(8,128)} %get-tuple-element.4) | data formatting | bytes 98304
  50.0 0.0 copy-done
  50.0 0.6 %copy.16 = f32[3,4,8,128]{3,2,1,0:T(8,128)} copy(f32[3,4,8,128]{3,2,1,0:T(8,128)S(1)} %copy-done) | data formatting | bytes 98304
Async XLA Ops:
  48.5 1.4 %copy-start = (f32[3,4,8,128]{3,2,1,0:T(8,128)S(1)}, f32[3,4,8,128]{3,2,1,0:T(8,128)}, u32[]{:S(2)}) copy-start(f32[3,4,8,128]{3,2,1,0:T(8,128)} %get-tuple-element.5) | copy-start | bytes 147460
